TPU v7x, 128 devices: a whole 4x4x4 slice. The times are simulated.
128 devices in a mesh: role: 8 (over z_hi, x), tp: 16 (over y, z_lo, core).
Axes of the slice: x: 4, y: 4, z: 4 (z_hi: 2, z_lo: 2; z = z_hi * 2 + z_lo), core: 2. Of those that a mesh axis runs over, the one named last changes fastest.
Arguments:
- text_embed: bfloat16 [8192, 8192], P('role', 'tp')
- vision_rows: bfloat16 [2048, 8192], P('role', 'tp'), may hold values from -6 to 6
- vision_group: int32 [2048], P('role'), may hold values from 0 to 7, as said below
- vision_slot: int32 [2048], P('role'), may hold values from 0 to 1023, as said below
- request_blocks: int32 [8, 8], P('role'), may hold values from 1 to 32, as said below
- ship_page: int32 [512], P('role'), may hold values from 0 to 16383, as said below
- paged_cache: bfloat16 [16384, 16, 2048], P(('role', 'tp')), may hold values from -6 to 6
- block_table: int32 [128, 256], P('role'), may hold values from -1 to 16383, as said below
- cache_len: int32 [128], P('role'), may hold values from 0 to 4096
- step_embed: bfloat16 [4, 128, 8192], P(None, 'role', 'tp')
- norm_gain: bfloat16 [8192], replicated, may hold values from 0.25 to 1.75
- query_weight: bfloat16 [8192, 8192], P(None, 'tp')
- keyvalue_weight: bfloat16 [8192, 2048], P(None, 'tp')
Outputs:
- prefill_out: bfloat16 [8192, 8192], P('role', 'tp')
- decode_out: bfloat16 [4, 128, 8192], P(None, 'role', 'tp')
Inputs may be any that keep to these rules, and one draw needn't show every extreme that they name: `vision_group`: of one group's 256 image rows at most 64 go to any one group, and one group receives exactly 64 from every group. `vision_slot`: image rows sent to one group have distinct positions. `request_blocks`: each row sums to 64; each group has one request of exactly 32 pages. `ship_page`: all named pages are distinct. Device number role * 16 + tp holds 128 consecutive pages. All pages of one request go to one group, and the requests of one group go to distinct groups (possibly its own), and of one group's 64 pages at most 2 go to any one device. `block_table`: rows of group h name only pages h * 2048 to (h + 1) * 2048 - 1, each of them exactly once over the group's rows; row r names its pages in order in its first ceil(cache_len[r] / 16) entries and -1 after them.
All inputs are finite; a program needn't handle non-finite values.
Results may differ from a plain program's by a relative error of at most 0.0055.
The roundings to bfloat16 on the way count: a program that leaves them out, or rounds other values in their place, can miss the bound.
Values may be sent and summed in bfloat16 or wider, within the bound.
No kernel may reach another device: no remote copies, remote signals or barrier semaphores. Data moves between devices by JAX's collectives and lax.ppermute only.
A program may use at most 256 MiB of HBM per device.

v0:
```python
import jax
import jax.numpy as jnp
from jax import lax
from jax.sharding import PartitionSpec as P

QUERY_HEADS = 64
KEYVALUE_HEADS = 8
HEAD_SIZE = 128
PAGE_TOKENS = 16


epsilon = 1e-06
masked_score = -1e30


def joined(part, axis, combine):
    gathered = jax.tree.map(lambda a: lax.all_gather(a, axis), part)

    def take(source):
        return jax.tree.map(lambda a: lax.dynamic_index_in_dim(a, source, 0, False), gathered)

    return lax.fori_loop(
        1, lax.axis_size(axis), lambda source, state: combine(state, take(source)), take(0)
    )


def spread_columns(columns_here):
    return lax.all_gather(columns_here, "tp", axis=1, tiled=True)


def project(row_block, norm_gain, query_weight, keyvalue_weight):
    gathered = lax.all_gather(row_block, "tp", axis=1, tiled=True)
    widened = gathered.astype(jnp.float32)
    mean_square = jnp.mean(widened * widened, axis=1, keepdims=True)
    normed = (
        widened * lax.rsqrt(mean_square + epsilon) * norm_gain.astype(jnp.float32)[None, :]
    ).astype(jnp.bfloat16)
    query_block = jnp.dot(normed, query_weight, preferred_element_type=jnp.float32)
    keyvalue_pairs = jnp.dot(normed, keyvalue_weight, preferred_element_type=jnp.float32)
    return (query_block.astype(jnp.bfloat16), keyvalue_pairs.astype(jnp.bfloat16))


def merge_states(first, second):
    joint_top = jnp.maximum(first[0], second[0])
    first_factor = jnp.exp(first[0] - joint_top)
    second_factor = jnp.exp(second[0] - joint_top)
    return (
        joint_top,
        first[1] * first_factor + second[1] * second_factor,
        first[2] * first_factor[..., None] + second[2] * second_factor[..., None],
    )


def per_device(
    text_embed,
    vision_rows,
    vision_group,
    vision_slot,
    request_blocks,
    ship_page,
    paged_cache,
    block_table,
    cache_len,
    step_embed,
    norm_gain,
    query_weight,
    keyvalue_weight,
):
    groups = lax.axis_size("role")
    width_tp = lax.axis_size("tp")
    column = lax.axis_index("tp")
    group_rows = text_embed.shape[0]
    score_scale = HEAD_SIZE ** (-0.5)
    group_extent = QUERY_HEADS // KEYVALUE_HEADS
    device_heads = query_weight.shape[1] // HEAD_SIZE
    kv_head = column * device_heads // group_extent
    image_count = vision_rows.shape[0]
    capacity = 2 * image_count // groups
    dest_hits = vision_group[:, None] == jnp.arange(groups, dtype=jnp.int32)[None, :]
    running = jnp.cumsum(dest_hits.astype(jnp.int32), axis=0) - 1
    rank_of = jnp.sum(jnp.where(dest_hits, running, 0), axis=1)
    slot_ids = jnp.arange(groups * capacity, dtype=jnp.int32)
    picked = (vision_group[None, :] == slot_ids[:, None] // capacity) & (
        rank_of[None, :] == slot_ids[:, None] % capacity
    )
    outgoing = jnp.dot(
        picked.astype(jnp.bfloat16), vision_rows, preferred_element_type=jnp.float32
    ).astype(jnp.bfloat16)
    out_slots = jnp.sum(jnp.where(picked, vision_slot[None, :] + 1, 0), axis=1) - 1
    arrived, arrived_slots = (
        lax.all_to_all(
            outgoing.reshape(groups, capacity, -1), "role", split_axis=0, concat_axis=0, tiled=True
        ),
        lax.all_to_all(
            out_slots.reshape(groups, capacity), "role", split_axis=0, concat_axis=0, tiled=True
        ),
    )
    positions = jnp.arange(group_rows, dtype=jnp.int32)
    landing = positions[:, None] == arrived_slots.reshape(1, -1)
    placed = jnp.dot(
        landing.astype(jnp.bfloat16),
        arrived.reshape(groups * capacity, -1),
        preferred_element_type=jnp.float32,
    ).astype(jnp.bfloat16)
    merged = jnp.where(jnp.any(landing, axis=1)[:, None], placed, text_embed)
    query_block, keyvalue_pairs = project(merged, norm_gain, query_weight, keyvalue_weight)
    every_pair = spread_columns(keyvalue_pairs)
    head_pair = lax.dynamic_slice_in_dim(every_pair, kv_head * 2 * HEAD_SIZE, 2 * HEAD_SIZE, 1)
    head_keys = head_pair[:, :HEAD_SIZE]
    head_values = head_pair[:, HEAD_SIZE:]
    request_ends = jnp.cumsum(request_blocks[0] * PAGE_TOKENS)
    segment = jnp.sum((positions[:, None] >= request_ends[None, :]).astype(jnp.int32), axis=1)
    allowed = (segment[:, None] == segment[None, :]) & (positions[None, :] <= positions[:, None])
    query_head_rows = query_block.reshape(group_rows, device_heads, HEAD_SIZE)
    scores = (
        jnp.einsum("chd,ud->hcu", query_head_rows, head_keys, preferred_element_type=jnp.float32)
        * score_scale
    )
    scores = jnp.where(allowed[None], scores, masked_score)
    row_top = jnp.max(scores, axis=-1, keepdims=True)
    weights = jnp.exp(scores - row_top)
    weights = (weights / jnp.sum(weights, axis=-1, keepdims=True)).astype(jnp.bfloat16)
    attended = jnp.einsum(
        "hcu,ud->chd", weights, head_values, preferred_element_type=jnp.float32
    ).astype(jnp.bfloat16)
    prefill_out = attended.reshape(group_rows, device_heads * HEAD_SIZE)
    device_pages = paged_cache.shape[0]
    blocks_here = ship_page.shape[0]
    slots_each = blocks_here // (2 * width_tp)
    dest_device = ship_page // device_pages
    dest_group = dest_device // width_tp
    mine = dest_device % width_tp == column
    group_hit = mine[:, None] & (
        dest_group[:, None] == jnp.arange(groups, dtype=jnp.int32)[None, :]
    )
    block_rank = jnp.sum(
        jnp.where(group_hit, jnp.cumsum(group_hit.astype(jnp.int32), axis=0) - 1, 0), axis=1
    )
    ship_ids = jnp.arange(groups * slots_each, dtype=jnp.int32)
    chosen = (
        mine[None, :]
        & (dest_group[None, :] == ship_ids[:, None] // slots_each)
        & (block_rank[None, :] == ship_ids[:, None] % slots_each)
    )
    parcels = jnp.dot(
        chosen.astype(jnp.bfloat16),
        every_pair.reshape(blocks_here, -1),
        preferred_element_type=jnp.float32,
    ).astype(jnp.bfloat16)
    parcel_pages = jnp.sum(jnp.where(chosen, ship_page[None, :] % device_pages + 1, 0), axis=1) - 1
    received, received_pages = (
        lax.all_to_all(
            parcels.reshape(groups, slots_each, -1), "role", split_axis=0, concat_axis=0, tiled=True
        ),
        lax.all_to_all(
            parcel_pages.reshape(groups, slots_each),
            "role",
            split_axis=0,
            concat_axis=0,
            tiled=True,
        ),
    )
    page_ids = jnp.arange(device_pages, dtype=jnp.int32)
    written = page_ids[:, None] == received_pages.reshape(1, -1)
    fresh_pages = jnp.dot(
        written.astype(jnp.bfloat16),
        received.reshape(groups * slots_each, -1),
        preferred_element_type=jnp.float32,
    ).astype(jnp.bfloat16)
    current_store = jnp.where(
        jnp.any(written, axis=1)[:, None], fresh_pages, paged_cache.reshape(device_pages, -1)
    )
    page_keyvalue = current_store.reshape(device_pages, PAGE_TOKENS, KEYVALUE_HEADS, 2, HEAD_SIZE)
    page_keys = page_keyvalue[:, :, :, 0, :]
    page_values = page_keyvalue[:, :, :, 1, :]
    first_page = (lax.axis_index("role") * width_tp + column) * device_pages
    page_match = block_table[None, :, :] == (first_page + page_ids)[:, None, None]
    owned = jnp.any(page_match, axis=2)
    entry_ids = jnp.arange(block_table.shape[1], dtype=jnp.int32)
    block_pos = jnp.sum(jnp.where(page_match, entry_ids[None, None, :], 0), axis=(1, 2))
    owner_len = jnp.sum(jnp.where(owned, cache_len[None, :], 0), axis=1)
    token_pos = block_pos[:, None] * PAGE_TOKENS + jnp.arange(PAGE_TOKENS, dtype=jnp.int32)[None, :]
    live_tokens = jnp.any(owned, axis=1)[:, None] & (token_pos < owner_len[:, None])
    owned_float = owned.astype(jnp.float32)
    owned_half = owned.astype(jnp.bfloat16)
    decoding_rows = block_table.shape[0]
    count_steps = step_embed.shape[0]
    own_start = column * device_heads
    highest = lax.Precision.HIGHEST
    query_own, pair_new = project(
        step_embed.reshape(count_steps * decoding_rows, -1),
        norm_gain,
        query_weight,
        keyvalue_weight,
    )
    merged_rows = spread_columns(jnp.concatenate([query_own, pair_new], axis=1)).reshape(
        count_steps, decoding_rows, width_tp, -1
    )
    query_all = merged_rows[:, :, :, : device_heads * HEAD_SIZE].reshape(
        count_steps, decoding_rows, QUERY_HEADS * HEAD_SIZE
    )
    new_page_stack = merged_rows[:, :, :, device_heads * HEAD_SIZE :].reshape(
        count_steps, decoding_rows, 2 * KEYVALUE_HEADS * HEAD_SIZE
    )
    page_query = (
        jnp.einsum("pb,sbf->spf", owned_half, query_all, preferred_element_type=jnp.float32)
        .astype(jnp.bfloat16)
        .reshape(count_steps, device_pages, KEYVALUE_HEADS, group_extent, HEAD_SIZE)
    )
    page_scores = (
        jnp.einsum("spkgd,ptkd->spkgt", page_query, page_keys, preferred_element_type=jnp.float32)
        * score_scale
    )
    live_here = live_tokens[None, :, None, None, :]
    page_scores = jnp.where(live_here, page_scores, masked_score)
    page_top = jnp.max(page_scores, axis=-1)
    row_best = jnp.max(
        jnp.where(owned[None, :, None, None, :], page_top[..., None], masked_score), axis=1
    )
    top_back = jnp.einsum("pb,skgb->spkg", owned_float, row_best, precision=highest)
    exponent = jnp.where(live_here, jnp.exp(page_scores - top_back[..., None]), 0.0)
    row_sum = jnp.einsum(
        "pb,spkg->skgb", owned_float, jnp.sum(exponent, axis=-1), precision=highest
    )
    page_acc = jnp.einsum(
        "spkgt,ptkd->spkgd",
        exponent.astype(jnp.bfloat16),
        page_values,
        preferred_element_type=jnp.float32,
    )
    row_acc = jnp.einsum("pb,spkgd->skgbd", owned_float, page_acc, precision=highest)
    heads_top = row_best.reshape(count_steps, QUERY_HEADS, decoding_rows)
    heads_sum = row_sum.reshape(count_steps, QUERY_HEADS, decoding_rows)
    heads_acc = row_acc.reshape(count_steps, QUERY_HEADS, decoding_rows, HEAD_SIZE)
    all_top, all_sum, all_acc = joined((heads_top, heads_sum, heads_acc), "tp", merge_states)
    mine_top = lax.dynamic_slice_in_dim(all_top, own_start, device_heads, 1)
    mine_sum = lax.dynamic_slice_in_dim(all_sum, own_start, device_heads, 1)
    mine_acc = lax.dynamic_slice_in_dim(all_acc, own_start, device_heads, 1)
    fresh_head = lax.dynamic_slice_in_dim(new_page_stack, kv_head * 2 * HEAD_SIZE, 2 * HEAD_SIZE, 2)
    own_query = query_own.reshape(count_steps, decoding_rows, device_heads, HEAD_SIZE)
    step_ids = jnp.arange(count_steps, dtype=jnp.int32)
    causal = (step_ids[None, :] <= step_ids[:, None])[:, None, None, :]
    new_scores = (
        jnp.einsum(
            "sbhd,tbd->shbt",
            own_query,
            fresh_head[:, :, :HEAD_SIZE],
            preferred_element_type=jnp.float32,
        )
        * score_scale
    )
    new_scores = jnp.where(causal, new_scores, masked_score)
    joint_top = jnp.maximum(mine_top, jnp.max(new_scores, axis=-1))
    carry_factor = jnp.exp(mine_top - joint_top)
    new_weights = jnp.where(causal, jnp.exp(new_scores - joint_top[..., None]), 0.0)
    denominator = mine_sum * carry_factor + jnp.sum(new_weights, axis=-1)
    combined = mine_acc * carry_factor[..., None] + jnp.einsum(
        "shbt,tbd->shbd",
        new_weights.astype(jnp.bfloat16),
        fresh_head[:, :, HEAD_SIZE:],
        preferred_element_type=jnp.float32,
    )
    result = (combined / denominator[..., None]).astype(jnp.bfloat16)
    decode_out = result.transpose(0, 2, 1, 3).reshape(
        count_steps, decoding_rows, device_heads * HEAD_SIZE
    )
    return (prefill_out, decode_out)


def solution(mesh):
    in_specs = (
        P("role", "tp"),
        P("role", "tp"),
        P("role"),
        P("role"),
        P("role", None),
        P("role"),
        P(("role", "tp"), None, None),
        P("role", None),
        P("role"),
        P(None, "role", "tp"),
        P(),
        P(None, "tp"),
        P(None, "tp"),
    )
    out_specs = (P("role", "tp"), P(None, "role", "tp"))
    return jax.shard_map(
        per_device, mesh=mesh, in_specs=in_specs, out_specs=out_specs, check_vma=False
    )
```

profile of v0, /device:TPU:1, one launch (start us, length us, event | category | flops | bytes accessed | tf_op | source)
XLA Modules:
  0.0 639.4 jit_solution(13086457734100743589)
XLA Ops:
  12.0 8.2 %all-to-all-start = ((s32[8,1,64]{2,1,0:T(1,128)}), s32[8,1,64]{2,1,0:T(1,128)S(1)}, u32[]{:S(2)}, u32[]{:S(2)}) async-start(s32[8,1,64]{2,1,0:T(1,128)} %sub.99), calls=%async_computation | async-start | bytes 8192 | tf_op jit(solution)/shard_map/all_to_all | solution.py:94
  20.1 2.1 convolution_convert_fusion.3
  22.2 4.3 all-to-all-done
  26.6 3.5 all-to-all-start.1
  31.7 8.1 %all-to-all-done.1 = bf16[8,64,512]{2,1,0:T(8,128)(2,1)S(1)} async-done(((bf16[8,64,512]{2,1,0:T(8,128)(2,1)}), bf16[8,64,512]{2,1,0:T(8,128)(2,1)S(1)}, u32[]{:S(2)}, u32[]{:S(2)}) %all-to-all-start.1) | async-done | bytes 524320 | tf_op jit(solution)/shard_map/all_to_all | solution.py:91
  39.7 2.9 fusion.46
  44.2 90.3 %all-gather.7.cloned.1.call-done = bf16[1024,8192]{1,0:T(8,128)(2,1)} async-done(((bf16[1024,512]{1,0:T(8,128)(2,1)}), bf16[1024,8192]{1,0:T(8,128)(2,1)}) %all-gather.7.cloned.1.call-update) | async-done | bytes 16777232 | tf_op jit(solution)/shard_map/all_gather | solution.py:32
  134.5 7.4 %fusion.5 = f32[1024]{0:T(1024)S(1)} fusion(bf16[1024,8192]{1,0:T(8,128)(2,1)} %all-gather.7.cloned.1.call-done), kind=kLoop, calls=%fused_computation.14 | loop fusion | flops 25164800 | bytes 16781312 | tf_op jit(solution)/shard_map/reduce_sum | solution.py:34
  142.0 3.2 copy-done.2
  145.2 5.4 fusion.47
  150.7 18.8 %all-gather.11.cloned.1.call-done = bf16[64,8192]{1,0:T(8,128)(2,1)} async-done(((bf16[64,512]{1,0:T(8,128)(2,1)}), bf16[64,8192]{1,0:T(8,128)(2,1)}) %all-gather.11.cloned.1.call-update) | async-done | bytes 1048592 | tf_op jit(solution)/shard_map/all_gather | solution.py:32
  169.4 1.5 fusion.33
  171.0 1.7 convolution_convert_fusion.5
  172.8 5.3 convolution_convert_fusion.4
  180.0 6.8 %all-to-all-start.2 = ((s32[8,1,2]{2,1,0:T(1,128)}), s32[8,1,2]{2,1,0:T(1,128)S(1)}, u32[]{:S(2)}, u32[]{:S(2)}) async-start(s32[8,1,2]{2,1,0:T(1,128)} %bitcast.16), calls=%async_computation.2 | async-start | bytes 8192 | tf_op jit(solution)/shard_map/all_to_all | solution.py:155
  186.8 2.6 fusion.36
  189.5 27.3 %all-gather.9.cloned.1.call-done = bf16[1024,2048]{1,0:T(8,128)(2,1)} async-done(((bf16[1024,128]{1,0:T(8,128)(2,1)}), bf16[1024,2048]{1,0:T(8,128)(2,1)}) %all-gather.9.cloned.1.call-update) | async-done | bytes 4194320 | tf_op jit(solution)/shard_map/all_gather | solution.py:28
  216.7 7.4 %reshape.400 = bf16[64,32768]{1,0:T(8,128)(2,1)} reshape(bf16[1024,2048]{1,0:T(8,128)(2,1)} %all-gather.9.cloned.1.call-done) | data formatting | bytes 8388608 | tf_op jit(solution)/shard_map/reshape | solution.py:147
  224.1 2.9 convolution_convert_fusion.1
  227.0 1.6 reshape.401
  228.6 6.3 all-to-all-start.3
  234.9 4.7 compare_reduce_fusion
  239.6 12.9 %copy.187 = bf16[16,8,16,2048]{3,1,2,0:T(8,128)(2,1)} copy(bf16[16,8,16,2048]{3,2,1,0:T(8,128)(2,1)} %bitcast.171) | data formatting | bytes 16777216
  254.3 3.0 all-gather.13.cloned.1.call-done
  259.8 1.7 reshape.407
  261.5 4.6 convolution_convert_fusion.2
  266.1 12.6 %copy.139 = bf16[4,128,8,8,128]{4,3,0,2,1:T(8,128)(2,1)} copy(bf16[4,128,8,8,128]{1,4,3,2,0:T(8,128)(2,1)} %bitcast.169) | data formatting | bytes 16777216 | tf_op jit(solution)/shard_map/reshape | solution.py:208
  279.2 9.0 %fusion.4 = bf16[128,32768]{1,0:T(8,128)(2,1)} fusion(bf16[128,32768]{1,0:T(8,128)(2,1)} %bitcast.168, bf16[16,32768]{1,0:T(8,128)(2,1)S(1)} %reshape.402, pred[128]{0:T(512)(128)(4,1)S(1)} %fusion.77, s32[16]{0:T(128)S(1)} %eq.197), kind=kOutput, calls=%fused_computation.12 | convolution fusion | flops 142608384 | bytes 17825984 | tf_op jit(solution)/shard_map/dot_general | solution.py:165
  288.2 14.4 %reshape.404 = bf16[128,16,8,2,128]{4,3,2,1,0:T(2,128)(2,1)} reshape(bf16[128,32768]{1,0:T(8,128)(2,1)} %fusion.4) | data formatting | bytes 16777216 | tf_op jit(solution)/shard_map/reshape | solution.py:173
  302.6 20.1 %fusion.105 = (bf16[128,16,8,1,128]{4,3,2,1,0:T(2,128)(2,1)}, bf16[128,16,8,1,128]{4,3,2,1,0:T(2,128)(2,1)}) fusion(bf16[128,16,8,2,128]{4,3,2,1,0:T(2,128)(2,1)} %reshape.404), kind=kLoop, calls=%fused_computation.180 | loop fusion | bytes 16777216 | tf_op jit(solution)/shard_map/slice | solution.py:175
  322.7 12.6 %bitcast_reduce_fusion = (f32[4,128,8,8]{3,0,2,1:T(4,128)S(1)}, f32[128,8,16,4,8]{2,4,3,1,0:T(8,128)}) fusion(pred[128,16]{1,0:T(8,128)(4,1)S(1)} %fusion.63, bf16[4,128,8,8,128]{4,3,0,2,1:T(8,128)(2,1)} %copy.139, bf16[128,16,8,1,128]{4,3,2,1,0:T(2,128)(2,1)} %get-tuple-element.227), kind=kOutput, calls=%fused_computation.18 | convolution fusion | flops 135757824 | bytes 14813184 | tf_op jit(solution)/shard_map/spkgd,ptkd->spkgt/dot_general | solution.py:211
  335.3 1.5 copy.140
  336.9 1.5 select_reduce_fusion
  339.3 2.3 copy.143
  341.6 4.3 copy.204
  346.0 15.6 %convolution_bitcast_fusion = f32[4,128,8,8,128]{4,3,0,2,1:T(8,128)} fusion(f32[128,8,16,4,8]{2,4,3,1,0:T(8,128)} %get-tuple-element.235, f32[4,128,8,8]{3,0,2,1:T(4,128)S(1)} %copy.143, pred[128,16]{1,0:T(8,128)(4,1)S(1)} %copy-done.7, bf16[128,16,8,128,1]{3,2,1,0,4:T(8,128)(2,1)S(1)} %bitcast.175), kind=kOutput, calls=%fused_computation.31 | convolution fusion | flops 136839168 | bytes 23201792 | tf_op jit(solution)/shard_map/spkgt,ptkd->spkgd/dot_general | solution.py:225
  361.6 21.5 %fusion.10 = f32[4,8,8,128,16]{3,4,2,1,0:T(8,128)} fusion(f32[4,128,8,8,128]{4,3,0,2,1:T(8,128)} %convolution_bitcast_fusion, pred[128,16]{1,0:T(8,128)(4,1)S(1)} %get-tuple-element.203), kind=kOutput, calls=%fused_computation.22 | convolution fusion | flops 805306368 | bytes 18876416 | tf_op jit(solution)/shard_map/pb,spkgd->skgbd/dot_general | solution.py:231
  386.8 1.6 fusion.32
  394.3 16.8 %fusion.41 = bf16[1024,512]{0,1:T(8,128)(2,1)} fusion(bf16[8192,512]{1,0:T(8,128)(2,1)} %param.26, bf16[1024,8192]{1,0:T(8,128)(2,1)} %all-gather.7.cloned.1.call-done, f32[8192]{0:T(1024)} %copy-done.5, f32[1024]{0:T(1024)} %copy-done.10), kind=kOutput, calls=%fused_computation.65 | convolution fusion | flops 8624013312 | bytes 26251264 | tf_op jit(solution)/shard_map/dot_general | solution.py:38
  411.0 10.6 %fusion.106 = (f32[4,1024]{1,0:T(4,128)S(1)}, f32[4,1024,1024]{1,2,0:T(8,128)}) fusion(pred[1024,1024]{0,1:T(8,128)(4,1)S(1)} %copy-done.3, bf16[1024,4,128]{0,2,1:T(8,128)(2,1)} %bitcast.186, bf16[1024,2048]{1,0:T(8,128)(2,1)} %all-gather.9.cloned.1.call-done, s32[]{:T(128)S(6)} %select_n.157), kind=kOutput, calls=%fused_computation.181 | convolution fusion | flops 1090520064 | bytes 19152900 | tf_op jit(solution)/shard_map/sub | solution.py:121
  421.7 7.5 %fusion.44 = bf16[128,4,1024]{2,0,1:T(8,128)(2,1)S(1)} fusion(f32[4,1024,1024]{1,2,0:T(8,128)} %get-tuple-element.233, f32[4,1024]{1,0:T(4,128)S(1)} %get-tuple-element.232, bf16[1024,2048]{1,0:T(8,128)(2,1)} %all-gather.9.cloned.1.call-done, s32[]{:T(128)S(6)} %add.239), kind=kOutput, calls=%fused_computation.66 | convolution fusion | flops 1082654720 | bytes 18104324 | tf_op jit(solution)/shard_map/hcu,ud->chd/dot_general | solution.py:123
  430.6 14.9 %fusion.14 = f32[4,128,8,8]{3,0,2,1:T(4,128)} fusion(f32[128,8,16,4,8]{2,4,3,1,0:T(8,128)} %get-tuple-element.235, f32[4,128,8,8]{3,0,2,1:T(4,128)S(1)} %copy.143, pred[128,16]{1,0:T(8,128)(4,1)S(1)} %copy-done.8), kind=kLoop, calls=%fused_computation.30 | loop fusion | flops 2588672 | bytes 2361344 | tf_op jit(solution)/shard_map/reduce_sum | solution.py:223
  445.5 2.0 copy.144
  447.8 22.1 %all-gather = f32[64,64,16]{1,2,0:T(8,128)S(1)} all-gather(f32[4,64,16]{1,2,0:T(8,128)S(1)} %fusion.58), channel_id=2, replica_groups=mesh['role'=8,'tp'=16] {'tp'}, dimensions={0}, use_global_device_ids=true | all-gather | bytes 278528 | tf_op jit(solution)/shard_map/all_gather | solution.py:17
  469.9 18.4 %all_gather.25 = f32[16,4,64,16]{2,3,1,0:T(8,128)S(1)} all-gather(f32[1,4,64,16]{2,3,1,0:T(8,128)S(1)} %copy.141), channel_id=1, replica_groups=mesh['role'=8,'tp'=16] {'tp'}, dimensions={0}, use_global_device_ids=true | all-gather | bytes 278528 | tf_op jit(solution)/shard_map/all_gather | solution.py:17
  488.3 76.9 %all-gather.15.cloned.1.call-done = f32[16,4,64,16,128]{4,3,2,1,0:T(8,128)} async-done(((f32[1,4,64,16,128]{4,3,2,1,0:T(8,128)}), f32[16,4,64,16,128]{4,3,2,1,0:T(8,128)}) %all-gather.15.cloned.1.call-update) | async-done | bytes 33554448 | tf_op jit(solution)/shard_map/all_gather | solution.py:17
  565.2 3.0 slice_bitcast_fusion
  568.2 60.4 %while.19 = (s32[]{:T(128)}, f32[4,64,16]{1,2,0:T(8,128)S(1)}, f32[4,64,16]{1,2,0:T(8,128)S(1)}, f32[4,64,16,128]{3,2,1,0:T(8,128)}, f32[16,4,64,16]{2,3,1,0:T(8...) while((s32[]{:T(128)}, f32[4,64,16]{1,2,0:T(8,128)S(1)}, ...), condition=%wide.region_23.24_spmd, body=%wide.region_22.23_spmd.sunk | while | flops 1597445 | bytes 6520983 | solution.py:22
  568.4 3.8 fusion.124
  572.5 3.8 fusion.124
  576.5 3.8 fusion.124
  580.5 3.8 fusion.124
  584.6 3.8 fusion.124
  588.6 3.8 fusion.124
  592.6 3.8 fusion.124
  596.6 3.8 fusion.124
  600.7 3.8 fusion.124
  604.7 3.8 fusion.124
  608.7 3.8 fusion.124
  612.7 3.8 fusion.124
  616.8 3.8 fusion.124
  620.8 3.8 fusion.124
  624.8 3.8 fusion.124
  629.3 2.3 copy.150
  (154 shorter events, 31.7 us)
Async XLA Ops:
  7.2 134.8 %copy-start = (bf16[8192,128]{1,0:T(8,128)(2,1)S(1)}, bf16[8192,128]{1,0:T(8,128)(2,1)}, u32[]{:S(2)}) copy-start(bf16[8192,128]{1,0:T(8,128)(2,1)} %param.27) | copy-start | bytes 6291460
  12.0 14.6 %all-to-all-start = ((s32[8,1,64]{2,1,0:T(1,128)}), s32[8,1,64]{2,1,0:T(1,128)S(1)}, u32[]{:S(2)}, u32[]{:S(2)}) async-start(s32[8,1,64]{2,1,0:T(1,128)} %sub.99), calls=%async_computation | async-start | bytes 8192 | tf_op jit(solution)/shard_map/all_to_all | solution.py:94
  26.6 13.2 %all-to-all-start.1 = ((bf16[8,64,512]{2,1,0:T(8,128)(2,1)}), bf16[8,64,512]{2,1,0:T(8,128)(2,1)S(1)}, u32[]{:S(2)}, u32[]{:S(2)}) async-start(bf16[8,64,512]{2,1,0:T(8,128)(2,1)} %bitcast.6), calls=%async_computation.1 | async-start | bytes 1048576 | tf_op jit(solution)/shard_map/all_to_all | solution.py:91
  30.1 104.4 %all-gather.7.cloned.1.call-start = ((), (), s32[]{:S(2)}) async-start(), calls=%async_computation.4 | async-start | bytes 17825792 | tf_op jit(solution)/shard_map/all_gather | solution.py:32
  42.7 126.7 %all-gather.11.cloned.1.call-start = ((), (), s32[]{:S(2)}) async-start(), calls=%async_computation.6 | async-start | bytes 1114112 | tf_op jit(solution)/shard_map/all_gather | solution.py:32
  43.4 173.3 %all-gather.9.cloned.1.call-start = ((), (), s32[]{:S(2)}) async-start(), calls=%async_computation.5 | async-start | bytes 4456448 | tf_op jit(solution)/shard_map/all_gather | solution.py:28
  44.2 128.5 %copy-start.5 = (f32[8192]{0:T(1024)}, f32[8192]{0:T(1024)S(1)}, u32[]{:S(2)}) copy-start(f32[8192]{0:T(1024)S(1)} %convert_element_type.85) | copy-start | bytes 98308
  134.5 10.7 %copy-start.2 = (bf16[1024,8192]{1,0:T(8,128)(2,1)S(1)}, bf16[1024,8192]{1,0:T(8,128)(2,1)}, u32[]{:S(2)}) copy-start(bf16[1024,8192]{1,0:T(8,128)(2,1)} %all-gather.7.cloned.1.call-done) | copy-start | bytes 50331652
  145.2 5.4 copy-start.10
  145.2 5.4 copy-start.13
  150.6 106.7 %all-gather.13.cloned.1.call-start = ((), (), s32[]{:S(2)}) async-start(), calls=%async_computation.7 | async-start | bytes 1392640 | tf_op jit(solution)/shard_map/all_gather | solution.py:28
  172.7 14.1 %copy-start.9 = (s32[16,256]{1,0:T(8,128)S(1)}, s32[16,256]{1,0:T(8,128)}, u32[]{:S(2)}) copy-start(s32[16,256]{1,0:T(8,128)} %param.22) | copy-start | bytes 49156
  178.1 38.6 %copy-start.4 = (bf16[64,512]{1,0:T(8,128)(2,1)}, bf16[64,512]{1,0:T(8,128)(2,1)S(1)}, u32[]{:S(2)}) copy-start(bf16[64,512]{1,0:T(8,128)(2,1)S(1)} %convolution_convert_fusion.4) | copy-start | bytes 196612
  180.0 48.6 %all-to-all-start.2 = ((s32[8,1,2]{2,1,0:T(1,128)}), s32[8,1,2]{2,1,0:T(1,128)S(1)}, u32[]{:S(2)}, u32[]{:S(2)}) async-start(s32[8,1,2]{2,1,0:T(1,128)} %bitcast.16), calls=%async_computation.2 | async-start | bytes 8192 | tf_op jit(solution)/shard_map/all_to_all | solution.py:155
  228.6 50.1 %all-to-all-start.3 = ((bf16[8,2,32768]{2,1,0:T(2,128)(2,1)}), bf16[8,2,32768]{2,1,0:T(2,128)(2,1)S(1)}, u32[]{:S(2)}, u32[]{:S(2)}) async-start(bf16[8,2,32768]{2,1,0:T(2,128)(2,1)} %reshape.401), calls=%async_computation.3 | async-start | bytes 2097152 | tf_op jit(solution)/shard_map/all_to_all | solution.py:152
  234.9 330.3 %all-gather.15.cloned.1.call-start = ((), (), s32[]{:S(2)}) async-start(), calls=%async_computation.8 | async-start | bytes 35651584 | tf_op jit(solution)/shard_map/all_gather | solution.py:17
  239.6 13.6 %copy-start.12 = (s32[16]{0:T(128)S(1)}, s32[16]{0:T(128)}, u32[]{:S(2)}) copy-start(s32[16]{0:T(128)} %param.23) | copy-start | bytes 196
  253.4 69.3 %copy-start.6 = (pred[128,16]{1,0:T(8,128)(4,1)}, pred[128,16]{1,0:T(8,128)(4,1)S(1)}, u32[]{:S(2)}) copy-start(pred[128,16]{1,0:T(8,128)(4,1)S(1)} %fusion.63) | copy-start | bytes 6148
  341.6 4.4 copy-start.7
  394.3 16.8 %copy-start.3 = (pred[1024,1024]{0,1:T(8,128)(4,1)S(1)}, pred[1024,1024]{0,1:T(8,128)(4,1)}, u32[]{:S(2)}) copy-start(pred[1024,1024]{0,1:T(8,128)(4,1)} %fusion.32) | copy-start | bytes 3145732
  421.7 8.9 %copy-start.8 = (pred[128,16]{1,0:T(8,128)(4,1)S(1)}, pred[128,16]{1,0:T(8,128)(4,1)}, u32[]{:S(2)}) copy-start(pred[128,16]{1,0:T(8,128)(4,1)} %copy-done.6) | copy-start | bytes 6148
  568.2 60.6 %copy-start.11 = (pred[4,4]{1,0:T(4,128)(4,1)S(1)}, pred[4,4]{1,0:T(4,128)(4,1)}, u32[]{:S(2)}) copy-start(pred[4,4]{1,0:T(4,128)(4,1)} %iota_compare_fusion.13) | copy-start | bytes 52
  628.6 4.1 copy-start.1
Sparse Core Ops, SparseCore 0:
  42.8 91.6 all-gather.6
  136.2 33.2 all-gather.10
  171.6 45.0 all-gather.8
  218.2 38.9 all-gather.12
  383.2 181.8 all-gather.14
where the time goes:
time: 649 us; the launch traced here: 639 us
  waiting for transfers between devices  229 us (35%)
  matrix products  121 us (19%)
  local copies, waits for them, and re-layouts  104 us (16%)
  other arithmetic  104 us (16%)
  blocking collectives  40.5 us (6%)
  starting transfers between devices  24.9 us (4%)
  between operations  14.4 us (2%)
    all_gather x2, waiting for transfers between devices, project(): gathered = lax.all_gather(row_block, 'tp', axis=1, tiled=True)  109 us
    all_gather x1, waiting for transfers between devices, joined(): gathered = jax.tree.map(lambda a: lax.all_gather(a, axis), part)  76.9 us
    add x15, other arithmetic, merge_states(): first[2] * first_factor[..., None] + second[2] * second_factor[..., None]  57 us
    all_gather x2, blocking collectives, joined(): gathered = jax.tree.map(lambda a: lax.all_gather(a, axis), part)  40.5 us
    all_gather x2, waiting for transfers between devices, spread_columns(): return lax.all_gather(columns_here, 'tp', axis=1, tiled=True)  30.2 us
    unnamed x35, local copies, waits for them, and re-layouts  24.2 us
    dot_general x2, matrix products, project(): jnp.dot(normed, query_weight, preferred_element_type=jnp.float32)  22.1 us
    dot_general x1, matrix products, per_device(): jnp.einsum('pb,spkgd->skgbd', owned_float, page_acc, precision=highest)  21.5 us
  transfers between devices with their start and end apart: 9, of which 7 were waited for; matrix products, arithmetic and copies ran while one was open for 23% of the time, Pallas kernels for 0%

commit v1 on v0

v1 whole, which is shorter than its diff:
```python
import jax
import jax.numpy as jnp
from jax import lax
from jax.experimental import pallas as pl
from jax.experimental.pallas import tpu as pltpu
from jax.sharding import PartitionSpec as P

HEAD_SIZE = 128
KV_HEADS = 8
PAGE_TOKENS = 16
EPS = 1e-06
LOW = -1e30
SCALE = HEAD_SIZE ** (-0.5)
BF = jnp.bfloat16
F32 = jnp.float32
VMEM_LIMIT = 56 * 2**20
TP = 16
ROLE = 8
STAT_ROWS = 16

CORE = 1
ZLO = 2
Y1 = 4
Y3 = 12


def params(**more):
    return pltpu.CompilerParams(vmem_limit_bytes=VMEM_LIMIT, **more)


def vmem():
    return pl.BlockSpec(memory_space=pltpu.VMEM)


def smem():
    return pl.BlockSpec(memory_space=pltpu.SMEM)


def hbm():
    return pl.BlockSpec(memory_space=pl.ANY)


def swap(x, axis, mask):
    size = TP if axis == "tp" else ROLE
    return lax.ppermute(x, axis, [(i, i ^ mask) for i in range(size)])


def ring_y(x):
    return lax.ppermute(
        x, "tp", [(i, (i + 4) % TP if i % 2 == 0 else (i - 4) % TP) for i in range(TP)]
    )


def doubling(x, axis, masks):
    held = x[None]
    for mask in masks:
        held = jnp.concatenate([held, swap(held, axis, mask)], axis=0)
    return held


def offsets(masks):
    table = [0]
    for mask in masks:
        table = table + [v ^ mask for v in table]
    return table


TP_MASKS = (CORE, ZLO, Y1, Y3)
ROLE_MASKS = (4, 1, 3)
TP_OFFSETS = offsets(TP_MASKS)
ROLE_OFFSETS = offsets(ROLE_MASKS)


def nt_dot(a, b):
    return lax.dot_general(a, b, (((1,), (1,)), ((), ())), preferred_element_type=F32)


def nn_dot(a, b):
    return jnp.dot(a, b, preferred_element_type=F32)


def eye(n):
    return lax.broadcasted_iota(jnp.int32, (n, n), 0) == lax.broadcasted_iota(
        jnp.int32, (n, n), 1
    )


def to_row(column):
    n = column.shape[0]
    return jnp.sum(jnp.where(eye(n), column, 0.0), axis=0, keepdims=True)


def to_column(row):
    n = row.shape[1]
    return jnp.sum(jnp.where(eye(n), row, 0.0), axis=1, keepdims=True)


def split3(x):
    high = x.astype(BF)
    rest = x - high.astype(F32)
    middle = rest.astype(BF)
    low = (rest - middle.astype(F32)).astype(BF)
    return high, middle, low


def stat_block(lse_column):
    row = to_row(lse_column)
    parts = jnp.concatenate(
        [row[:, :128], row[:, 128:], jnp.zeros((6, 128), F32)], axis=0
    )
    high, middle, low = split3(parts)
    return jnp.concatenate(
        [
            high[:2].astype(F32),
            middle[:2].astype(F32),
            low[:2].astype(F32),
            jnp.zeros((10, 128), F32),
        ],
        axis=0,
    ).astype(BF)


def stat_column(block):
    wide = block.astype(F32)
    rows = wide[0:2] + wide[2:4] + wide[4:6]
    return jnp.concatenate([to_column(rows[0:1]), to_column(rows[1:2])], axis=0)


def step_kernel(order, xs, gain, wq, wa, wb, q_out, a_out, b_out, scale, acc):
    i = pl.program_id(0)

    @pl.when(i == 0)
    def _():
        total = jnp.zeros((xs.shape[1], 1), F32)
        for k in range(TP):
            wide = xs[k].astype(F32)
            total = total + jnp.sum(wide * wide, axis=1, keepdims=True)
        scale[...] = jnp.broadcast_to(
            lax.rsqrt(total / (TP * xs.shape[2]) + EPS), scale.shape
        )
        acc[...] = jnp.zeros_like(acc)

    normed = (xs[i].astype(F32) * scale[:, :1] * gain[0].astype(F32)).astype(BF)
    acc[:, :512] += nn_dot(normed, wq[...])
    acc[:, 512:640] += nn_dot(normed, wa[...])
    acc[:, 640:768] += nn_dot(normed, wb[...])

    @pl.when(i == TP - 1)
    def _():
        q_out[...] = acc[:, :512].astype(BF)
        a_out[...] = acc[:, 512:640].astype(BF)
        b_out[...] = acc[:, 640:768].astype(BF)


def step_project(order, xs, gain, wq, wa, wb):
    rows = xs.shape[1]
    return pl.pallas_call(
        step_kernel,
        grid_spec=pltpu.PrefetchScalarGridSpec(
            num_scalar_prefetch=1,
            grid=(TP,),
            in_specs=[
                pl.BlockSpec(xs.shape, lambda i, o: (0, 0, 0)),
                pl.BlockSpec((1, 1, 512), lambda i, o: (o[i], 0, 0)),
                pl.BlockSpec((512, 512), lambda i, o: (o[i], 0)),
                pl.BlockSpec((512, 128), lambda i, o: (o[i], 0)),
                pl.BlockSpec((512, 128), lambda i, o: (o[i], 0)),
            ],
            out_specs=[
                pl.BlockSpec((rows, 512), lambda i, o: (0, 0)),
                pl.BlockSpec((rows, 128), lambda i, o: (0, 0)),
                pl.BlockSpec((rows, 128), lambda i, o: (0, 0)),
            ],
            scratch_shapes=[pltpu.VMEM((rows, 128), F32), pltpu.VMEM((rows, 768), F32)],
        ),
        out_shape=[
            jax.ShapeDtypeStruct((rows, 512), BF),
            jax.ShapeDtypeStruct((rows, 128), BF),
            jax.ShapeDtypeStruct((rows, 128), BF),
        ],
        compiler_params=params(),
        cost_estimate=pl.CostEstimate(
            flops=2 * rows * 8192 * 768, bytes_accessed=14 * 2**20, transcendentals=0
        ),
        name="step_project",
    )(order, xs, gain.reshape(TP, 1, 512), wq, wa, wb)


def project_kernel(first, last, counts, *refs):
    blocks = sum(counts)
    refs = list(refs)
    index = refs.pop(0)
    core = refs.pop(0)
    tops = [refs.pop(0) for _ in counts]
    lows = [refs.pop(0) for _ in counts]
    ssq, gain, wq, wa, wb = [refs.pop(0) for _ in range(5)]
    acc_in = None if first else refs.pop(0)
    if last:
        q_out, k_out, v_out = [refs.pop(0) for _ in range(3)]
    else:
        acc_out = refs.pop(0)
    xbuf, wbuf, acc, scale, xsem, wsem, asem = refs
    half = xbuf.shape[2]

    copies = []
    place = 0
    for top, low, count in zip(tops, lows, counts):
        for n in range(count):
            start = pl.multiple_of(index[place] * 512, 512)
            rows = pl.ds(start, 512)
            here = [
                pltpu.make_async_copy(top.at[n], xbuf.at[place, 0], xsem.at[place, 0]),
                pltpu.make_async_copy(low.at[n], xbuf.at[place, 1], xsem.at[place, 1]),
                pltpu.make_async_copy(
                    wq.at[rows], wbuf.at[place, :, pl.ds(0, 512)], wsem.at[place, 0]
                ),
                pltpu.make_async_copy(
                    wa.at[rows], wbuf.at[place, :, pl.ds(512, 128)], wsem.at[place, 1]
                ),
                pltpu.make_async_copy(
                    wb.at[rows], wbuf.at[place, :, pl.ds(640, 128)], wsem.at[place, 2]
                ),
            ]
            for copy in here:
                copy.start()
            copies.append(here)
            place += 1
    if not first:
        load = pltpu.make_async_copy(acc_in, acc, asem.at[0])
        load.start()

    total = jnp.zeros((8, 128), F32)
    for k in range(TP):
        wide = ssq[k].astype(F32)
        total = total + (wide[0:8] + wide[8:16] + wide[16:24])
    factor = lax.rsqrt(total / (TP * 512) + EPS)
    for n in range(8):
        scale[n * 128 : (n + 1) * 128, :] = jnp.broadcast_to(
            to_column(factor[n : n + 1]), (128, 128)
        )
    if not first:
        load.wait()

    for place in range(blocks):
        for copy in copies[place]:
            copy.wait()
        gain_row = gain[index[place]].astype(F32)
        weights = wbuf.at[place]

        def tile(n, carry, place=place, gain_row=gain_row, weights=weights):
            part = n // (half // 256)
            at = pl.multiple_of((n % (half // 256)) * 256, 256)
            row = pl.multiple_of(n * 256, 256)
            x = xbuf[place, part, pl.ds(at, 256), :].astype(F32)
            normed = (x * scale[pl.ds(row, 256), :1] * gain_row).astype(BF)
            product = nn_dot(normed, weights[...])
            if first and place == 0:
                acc[pl.ds(row, 256), :] = product
            else:
                acc[pl.ds(row, 256), :] += product
            return carry

        lax.fori_loop(0, 2 * half // 256, tile, 0)

    if last:
        q_out[...] = acc[:, :512].astype(BF)
        own = acc[:, 512:640]
        other = acc[:, 640:768]
        k_out[...] = jnp.where(core[0] == 0, own, other).astype(BF)
        v_out[...] = jnp.where(core[0] == 0, other, own).astype(BF)
    else:
        store = pltpu.make_async_copy(acc, acc_out, asem.at[0])
        store.start()
        store.wait()


def project(index, core, tops, lows, ssq, gain, wq, wa, wb, acc, last):
    first = acc is None
    counts = tuple(a.shape[0] for a in tops)
    blocks = sum(counts)
    half = tops[0].shape[1]
    rows = 2 * half
    args = [index, core, *tops, *lows, ssq, gain.reshape(TP, 1, 512), wq, wa, wb]
    specs = [smem(), smem()] + [hbm()] * (2 * len(counts)) + [vmem(), vmem()] + [hbm()] * 3
    if not first:
        args.append(acc)
        specs.append(hbm())
    if last:
        shapes = [
            jax.ShapeDtypeStruct((rows, 512), BF),
            jax.ShapeDtypeStruct((rows, 128), BF),
            jax.ShapeDtypeStruct((rows, 128), BF),
        ]
        out_specs = [vmem()] * 3
    else:
        shapes = jax.ShapeDtypeStruct((rows, 768), F32)
        out_specs = hbm()

    def body(*refs):
        project_kernel(first, last, counts, *refs)

    return pl.pallas_call(
        body,
        in_specs=specs,
        out_specs=out_specs,
        out_shape=shapes,
        scratch_shapes=[
            pltpu.VMEM((blocks, 2, half, 512), BF),
            pltpu.VMEM((blocks, 512, 768), BF),
            pltpu.VMEM((rows, 768), F32),
            pltpu.VMEM((rows, 128), F32),
            pltpu.SemaphoreType.DMA((blocks, 2)),
            pltpu.SemaphoreType.DMA((blocks, 3)),
            pltpu.SemaphoreType.DMA((1,)),
        ],
        compiler_params=params(),
        cost_estimate=pl.CostEstimate(
            flops=2 * rows * 512 * blocks * 768,
            bytes_accessed=blocks * 2 * 2**20,
            transcendentals=0,
        ),
        name="prefill_project",
    )(*args)


def paged_kernel(first_chunk, slot_page, slot_live, where, q, cache, out, kv, top, total, acc, lse):
    lane = lax.broadcasted_iota(jnp.int32, (1, 128), 1)

    def one_row(r, carry):
        top[...] = jnp.full_like(top, LOW)
        total[...] = jnp.zeros_like(total)
        acc[...] = jnp.zeros_like(acc)
        at = pl.multiple_of(r * 16, 16)

        def one_chunk(i, inner):
            live = jnp.zeros((1, 128), jnp.int32)
            for j in range(8):
                slot = i * 8 + j
                kv[j * 16 : (j + 1) * 16, :] = cache[slot_page[slot]]
                live = jnp.where(lane // PAGE_TOKENS == j, slot_live[slot], live)
            valid = lane % PAGE_TOKENS < live
            for k in range(KV_HEADS):
                keys = kv[:, k * 256 : k * 256 + 128]
                values = kv[:, k * 256 + 128 : k * 256 + 256]
                queries = jnp.concatenate(
                    [
                        q[where[2 * k], pl.ds(at, 16), :],
                        q[where[2 * k + 1], pl.ds(at, 16), :],
                    ],
                    axis=0,
                )
                rows = slice(k * 32, (k + 1) * 32)
                scores = jnp.where(valid, nt_dot(queries, keys) * SCALE, LOW)
                old = top[rows, :]
                new = jnp.maximum(old, jnp.max(scores, axis=1, keepdims=True))
                weights = jnp.where(valid, jnp.exp(scores - new), 0.0)
                fade = jnp.exp(old - new)
                top[rows, :] = new
                total[rows, :] = total[rows, :] * fade + jnp.sum(weights, axis=1, keepdims=True)
                acc[rows, :] = acc[rows, :] * fade + nn_dot(weights.astype(BF), values)
            return inner

        lax.fori_loop(first_chunk[r], first_chunk[r + 1], one_chunk, 0)
        some = total[...] > 0.0
        divisor = jnp.where(some, total[...], 1.0)
        result = (acc[...] / divisor).astype(BF)
        level = jnp.where(some, top[...] + jnp.log(divisor), LOW)
        for t in range(TP):
            out[t, pl.ds(at, 16), :] = result[t * 16 : (t + 1) * 16]
            lse[t, pl.ds(at, 16), :] = level[t * 16 : (t + 1) * 16]
        return carry

    lax.fori_loop(0, 16, one_row, 0)

    def one_target(t, carry):
        out[t, 256:272, :] = stat_block(lse[t][:, :1])
        return carry

    lax.fori_loop(0, TP, one_target, 0)


def paged_attention(first_chunk, slot_page, slot_live, where, q, cache):
    return pl.pallas_call(
        paged_kernel,
        in_specs=[smem()] * 4 + [vmem()] * 2,
        out_specs=vmem(),
        out_shape=jax.ShapeDtypeStruct((TP, 256 + STAT_ROWS, 128), BF),
        scratch_shapes=[
            pltpu.VMEM((128, 2048), BF),
            pltpu.VMEM((256, 128), F32),
            pltpu.VMEM((256, 128), F32),
            pltpu.VMEM((256, 128), F32),
            pltpu.VMEM((TP, 256, 128), F32),
        ],
        compiler_params=params(),
        cost_estimate=pl.CostEstimate(
            flops=2 * 10**9, bytes_accessed=12 * 2**20, transcendentals=2**20
        ),
        name="paged_attention",
    )(first_chunk, slot_page, slot_live, where, q, cache)


def fresh_kernel(group, q, keys, values, token_row, out):
    def one_group(i, carry):
        queries = q[i]
        row = lax.broadcasted_iota(jnp.int32, (256, 1), 0) // 16 + i * 16
        valid = token_row[...] == row
        scores = jnp.where(valid, nt_dot(queries, keys[...]) * SCALE, LOW)
        top = jnp.max(scores, axis=1, keepdims=True)
        weights = jnp.where(valid, jnp.exp(scores - top), 0.0)
        total = jnp.sum(weights, axis=1, keepdims=True)
        acc = nn_dot(weights.astype(BF), values[...])
        some = total > 0.0
        divisor = jnp.where(some, total, 1.0)
        target = group[i]
        out[target, :256, :] = (acc / divisor).astype(BF)
        out[target, 256:272, :] = stat_block(jnp.where(some, top + jnp.log(divisor), LOW))
        return carry

    lax.fori_loop(0, ROLE, one_group, 0)


def fresh_attention(group, q, keys, values, token_row):
    return pl.pallas_call(
        fresh_kernel,
        in_specs=[smem()] + [vmem()] * 4,
        out_specs=vmem(),
        out_shape=jax.ShapeDtypeStruct((ROLE, 256 + STAT_ROWS, 128), BF),
        compiler_params=params(),
        cost_estimate=pl.CostEstimate(
            flops=10**9, bytes_accessed=2 * 2**20, transcendentals=2**21
        ),
        name="fresh_attention",
    )(group, q, keys, values, token_row)


def prefill_kernel(q, keys, values, seg_row, out):
    rows = q.shape[0]
    for tile in range(rows // 256):
        high = (tile + 1) * 256
        low = max(0, (tile * 256 - 511) // 256 * 256)
        span = high - low
        seg_keys = seg_row[:, low:high]
        seg_queries = to_column(seg_row[:, tile * 256 : high])
        row = lax.broadcasted_iota(jnp.int32, (256, span), 0) + tile * 256
        column = lax.broadcasted_iota(jnp.int32, (256, span), 1) + low
        valid = (seg_keys == seg_queries) & (column <= row)
        for h in range(4):
            lanes = slice(h * 128, (h + 1) * 128)
            scores = nt_dot(q[tile * 256 : high, lanes], keys[low:high, :]) * SCALE
            scores = jnp.where(valid, scores, LOW)
            top = jnp.max(scores, axis=1, keepdims=True)
            weights = jnp.exp(scores - top)
            total = jnp.sum(weights, axis=1, keepdims=True)
            weights = (weights * (1.0 / total)).astype(BF)
            out[tile * 256 : high, lanes] = nn_dot(weights, values[low:high, :]).astype(BF)


def prefill_attention(q, keys, values, seg_row):
    return pl.pallas_call(
        prefill_kernel,
        in_specs=[vmem()] * 4,
        out_specs=vmem(),
        out_shape=jax.ShapeDtypeStruct(q.shape, BF),
        compiler_params=params(),
        cost_estimate=pl.CostEstimate(
            flops=3 * 10**9, bytes_accessed=3 * 2**20, transcendentals=3 * 2**20
        ),
        name="prefill_attention",
    )(q, keys, values, seg_row)


def merge_kernel(held, fresh, q, new_keys, new_values, out):
    queries = q[...]
    row = lax.broadcasted_iota(jnp.int32, (256, 64), 0)
    key = lax.broadcasted_iota(jnp.int32, (256, 64), 1)
    valid = (row // 16 == key % 16) & (key // 16 <= row % 16 // 4)
    scores = jnp.where(valid, nt_dot(queries, new_keys[...]) * SCALE, LOW)
    top = jnp.max(scores, axis=1, keepdims=True)
    levels = []
    for source, count in ((held, TP), (fresh, ROLE)):
        for n in range(count):
            levels.append(stat_column(source[n, 256:272, :]))
    for level in levels:
        top = jnp.maximum(top, level)
    weights = jnp.where(valid, jnp.exp(scores - top), 0.0)
    total = jnp.sum(weights, axis=1, keepdims=True)
    acc = nn_dot(weights.astype(BF), new_values[...])
    place = 0
    for source, count in ((held, TP), (fresh, ROLE)):
        for n in range(count):
            factor = jnp.exp(levels[place] - top)
            total = total + factor
            acc = acc + source[n, :256, :].astype(F32) * factor
            place += 1
    out[...] = (acc / total).astype(BF)


def merge(held, fresh, q, new_keys, new_values):
    return pl.pallas_call(
        merge_kernel,
        in_specs=[vmem()] * 5,
        out_specs=vmem(),
        out_shape=jax.ShapeDtypeStruct((256, 128), BF),
        compiler_params=params(),
        cost_estimate=pl.CostEstimate(
            flops=10**7, bytes_accessed=2 * 2**20, transcendentals=2**16
        ),
        name="decode_merge",
    )(held, fresh, q, new_keys, new_values)


def page_tables(block_table, cache_len, ships, first_page):
    pages = 128
    page_ids = jnp.arange(pages, dtype=jnp.int32)
    rows, entries = block_table.shape
    code_of = (
        jnp.arange(rows, dtype=jnp.int32)[:, None] * entries
        + jnp.arange(entries, dtype=jnp.int32)[None, :]
    )
    match = block_table[None] == (first_page + page_ids)[:, None, None]
    code = jnp.max(jnp.where(match, code_of[None], -1), axis=(1, 2))
    replaced = jnp.any(ships.reshape(1, -1) == (first_page + page_ids)[:, None], axis=1)
    row = jnp.where(replaced | (code < 0), rows, code // entries)
    onehot = row[:, None] == jnp.arange(rows, dtype=jnp.int32)[None, :]
    length = jnp.sum(jnp.where(onehot, cache_len[None, :], 0), axis=1)
    live = jnp.clip(length - (code % entries) * PAGE_TOKENS, 0, PAGE_TOKENS)
    count = jnp.sum(onehot.astype(jnp.int32), axis=0)
    chunks = (count + 7) // 8
    ids17 = jnp.arange(rows + 1, dtype=jnp.int32)
    ids16 = jnp.arange(rows, dtype=jnp.int32)
    first_chunk = jnp.sum(
        jnp.where(ids16[None, :] < ids17[:, None], chunks[None, :], 0), axis=1
    )
    rank = jnp.sum(
        ((row[None, :] == row[:, None]) & (page_ids[None, :] < page_ids[:, None])).astype(jnp.int32),
        axis=1,
    )
    base = jnp.sum(jnp.where(onehot, first_chunk[None, :rows], 0), axis=1)
    slot = jnp.where(row < rows, base * 8 + rank, -1)
    hit = slot[None, :] == jnp.arange(256, dtype=jnp.int32)[:, None]
    slot_page = jnp.sum(jnp.where(hit, page_ids[None, :], 0), axis=1)
    slot_live = jnp.sum(jnp.where(hit, live[None, :], 0), axis=1)
    return first_chunk, slot_page, slot_live


def token_rows(tables, lengths, ship_page):
    rows, entries = tables.shape
    code_of = (
        jnp.arange(rows, dtype=jnp.int32)[:, None] * entries
        + jnp.arange(entries, dtype=jnp.int32)[None, :]
    )
    match = tables[None] == ship_page[:, None, None]
    code = jnp.max(jnp.where(match, code_of[None], -1), axis=(1, 2))
    row = code // entries
    onehot = row[:, None] == jnp.arange(rows, dtype=jnp.int32)[None, :]
    length = jnp.sum(jnp.where(onehot, lengths[None, :], 0), axis=1)
    live = jnp.where(code >= 0, length - (code % entries) * PAGE_TOKENS, 0)
    token = jnp.arange(PAGE_TOKENS, dtype=jnp.int32)[None, :]
    return jnp.where(token < live[:, None], row[:, None], -1).reshape(1, -1)


def per_device(
    text_embed,
    vision_rows,
    vision_group,
    vision_slot,
    request_blocks,
    ship_page,
    paged_cache,
    block_table,
    cache_len,
    step_embed,
    norm_gain,
    query_weight,
    keyvalue_weight,
):
    column = lax.axis_index("tp")
    role = lax.axis_index("role")
    core = column % 2
    group_rows, width = text_embed.shape
    half = group_rows // 2
    steps, rows, _ = step_embed.shape

    meta = jnp.concatenate(
        [
            block_table.reshape(-1),
            cache_len,
            ship_page,
            jnp.zeros((48,), jnp.int32),
        ]
    ).reshape(33, 128)
    metas = doubling(meta, "role", ROLE_MASKS).reshape(ROLE, -1)
    tables = metas[:, :4096].reshape(ROLE * rows, -1)
    lengths = metas[:, 4096 : 4096 + rows].reshape(-1)
    ships = metas[:, 4112 : 4112 + 64]

    image_count = vision_rows.shape[0]
    capacity = 2 * image_count // ROLE
    dest_hits = vision_group[:, None] == jnp.arange(ROLE, dtype=jnp.int32)[None, :]
    running = jnp.cumsum(dest_hits.astype(jnp.int32), axis=0) - 1
    rank_of = jnp.sum(jnp.where(dest_hits, running, 0), axis=1)
    slot_ids = jnp.arange(ROLE * capacity, dtype=jnp.int32)
    picked = (vision_group * capacity + rank_of)[None, :] == slot_ids[:, None]
    outgoing = nn_dot(picked.astype(BF), vision_rows).astype(BF)
    out_slots = jnp.sum(jnp.where(picked, vision_slot[None, :] + 1, 0), axis=1) - 1
    slot_rows = jnp.stack([out_slots // 32, out_slots % 32], axis=0).astype(BF)
    slot_rows = jnp.broadcast_to(
        jnp.concatenate([slot_rows, jnp.zeros((14, ROLE * capacity), BF)], axis=0)[None],
        (ROLE, 16, ROLE * capacity),
    )
    message = jnp.concatenate([outgoing.reshape(ROLE, capacity, width), slot_rows], axis=1)
    arrived = lax.all_to_all(message, "role", split_axis=0, concat_axis=0, tiled=True)
    slot_parts = lax.dynamic_slice_in_dim(
        arrived[:, capacity : capacity + 2, :], role * capacity, capacity, 2
    ).astype(jnp.int32)
    arrived_slots = (slot_parts[:, 0] * 32 + slot_parts[:, 1]).reshape(1, -1)
    arrived_rows = arrived[:, :capacity, :].reshape(ROLE * capacity, width)
    positions = jnp.arange(group_rows, dtype=jnp.int32)

    def merged_rows(low, high):
        landing = positions[low:high, None] == arrived_slots
        placed = nn_dot(landing.astype(BF), arrived_rows).astype(BF)
        return jnp.where(jnp.any(landing, axis=1)[:, None], placed, text_embed[low:high])

    top_own = merged_rows(0, half)
    low_own = merged_rows(half, group_rows)

    def partial_squares(block):
        wide = block.astype(F32)
        return jnp.sum(wide * wide, axis=1)

    other_weight = swap(keyvalue_weight, "tp", CORE)
    tp_order = column ^ jnp.array(TP_OFFSETS, jnp.int32)
    steps_all = doubling(step_embed.reshape(steps * rows, width), "tp", TP_MASKS)
    step_q, step_a, step_b = step_project(
        tp_order, steps_all, norm_gain, query_weight, keyvalue_weight, other_weight
    )
    new_keys = jnp.where(core == 0, step_a, step_b)
    new_values = jnp.where(core == 0, step_b, step_a)
    own_queries = (
        step_q.reshape(steps, rows, 4, HEAD_SIZE).transpose(1, 0, 2, 3).reshape(rows * 16, HEAD_SIZE)
    )

    def plus(a):
        return swap(a, "tp", CORE)

    top_pair = jnp.stack([top_own, plus(top_own)])
    low_pair = jnp.stack([low_own, plus(low_own)])
    top_z_own = swap(top_own, "tp", ZLO)
    low_y = ring_y(low_pair)
    top_y = ring_y(top_pair)
    low_z_own = swap(low_own, "tp", ZLO)
    top_z = jnp.stack([top_z_own, plus(top_z_own)])
    low_z = jnp.stack([low_z_own, plus(low_z_own)])
    top_zy = ring_y(top_z)
    low_zy = swap(low_y, "tp", ZLO)
    far = ring_y(jnp.stack([low_y[0], top_y[0]]))
    top_zf_own = ring_y(top_zy[0])
    low_zf_own = swap(far[0], "tp", ZLO)
    far_other = plus(far)

    squares = jnp.concatenate([partial_squares(top_own), partial_squares(low_own)]).reshape(8, 128)
    reduced = lax.reduce_precision(squares, 8, 7)
    rest = squares - reduced
    reduced2 = lax.reduce_precision(rest, 8, 7)
    square_parts = jnp.concatenate(
        [reduced, reduced2, rest - reduced2, jnp.zeros((8, 128), F32)], axis=0
    ).astype(BF)
    query_message = jnp.concatenate([own_queries, square_parts], axis=0)
    query_all = doubling(query_message, "tp", TP_MASKS)
    ssq = query_all[:, 256:288, :]
    queries_role = doubling(own_queries, "role", ROLE_MASKS)

    y = column // 4
    low_bits = column % 4

    def at(dy, bits):
        return ((y + dy) % 4) * 4 + (low_bits ^ bits)

    toward = jnp.where(core == 0, -1, 1)
    index_1 = jnp.stack(
        [
            at(0, 0),
            at(0, 1),
            at(0, 2),
            at(0, 3),
            at(toward, 0),
            at(toward, 1),
            at(-toward, 1),
            at(-toward, 0),
        ]
    )
    index_2 = jnp.stack(
        [at(toward, 2), at(toward, 3), at(-toward, 3), at(-toward, 2), at(2, 0), at(2, 1)]
    )
    index_3 = jnp.stack([at(2, 2), at(2, 3)])
    core_id = core.reshape(1)
    weights = (norm_gain, query_weight, keyvalue_weight, other_weight)
    acc = project(
        index_1,
        core_id,
        [top_pair, top_z, top_y, plus(top_y)],
        [low_pair, low_z, low_y, plus(low_y)],
        ssq,
        *weights,
        None,
        False,
    )
    acc = project(
        index_2,
        core_id,
        [top_zy, plus(top_zy), far[1:], far_other[1:]],
        [low_zy, plus(low_zy), far[:1], far_other[:1]],
        ssq,
        *weights,
        acc,
        False,
    )
    q_rows, keys, values = project(
        index_3,
        core_id,
        [top_zf_own[None], plus(top_zf_own)[None]],
        [low_zf_own[None], plus(low_zf_own)[None]],
        ssq,
        *weights,
        acc,
        True,
    )

    first_page = (role * TP + column) * 128
    first_chunk, slot_page, slot_live = page_tables(block_table, cache_len, ships, first_page)
    difference = column ^ jnp.arange(TP, dtype=jnp.int32)
    far_bit = difference // 8
    near_bit = (difference // 4) % 2 ^ far_bit
    where = difference % 4 + 4 * near_bit + 8 * far_bit
    held = paged_attention(
        first_chunk, slot_page, slot_live, where, query_all[:, :256, :], paged_cache
    )
    held_parts = lax.all_to_all(held, "tp", split_axis=0, concat_axis=0, tiled=True)

    token_row = token_rows(tables, lengths, ship_page)
    role_order = role ^ jnp.array(ROLE_OFFSETS, jnp.int32)
    fresh = fresh_attention(role_order, queries_role, keys, values, token_row)
    fresh_parts = lax.all_to_all(fresh, "role", split_axis=0, concat_axis=0, tiled=True)

    request_ends = jnp.cumsum(request_blocks[0] * PAGE_TOKENS)
    segment = jnp.sum((positions[:, None] >= request_ends[None, :]).astype(F32), axis=1)
    prefill_out = prefill_attention(q_rows, keys, values, segment.reshape(1, -1))

    decode = merge(held_parts, fresh_parts, own_queries, new_keys, new_values)
    decode_out = (
        decode.reshape(rows, steps, 4, HEAD_SIZE).transpose(1, 0, 2, 3).reshape(steps, rows, 512)
    )
    return (prefill_out, decode_out)


def solution(mesh):
    in_specs = (
        P("role", "tp"),
        P("role", "tp"),
        P("role"),
        P("role"),
        P("role", None),
        P("role"),
        P(("role", "tp"), None, None),
        P("role", None),
        P("role"),
        P(None, "role", "tp"),
        P(),
        P(None, "tp"),
        P(None, "tp"),
    )
    out_specs = (P("role", "tp"), P(None, "role", "tp"))
    return jax.shard_map(
        per_device, mesh=mesh, in_specs=in_specs, out_specs=out_specs, check_vma=False
    )
```

time: 649 us -> 295 us (0.45)
  the two profiles are of different devices: /device:TPU:1 before, /device:TPU:10 now
where the time goes in v1:
time: 295 us; the launch traced here: 291 us
  Pallas kernels  135 us (46%)
  starting transfers between devices  58.5 us (20%)
  waiting for transfers between devices  44.5 us (15%)
  other arithmetic  26 us (9%)
  local copies, waits for them, and re-layouts  22.2 us (8%)
  matrix products  4.08 us (1%)
    pallas_call x1, Pallas kernels, paged_attention(): pl.pallas_call(paged_kernel, in_specs=[smem()] * 4 + [vmem()] * 2, out_sp...  52.9 us
    pallas_call x3, Pallas kernels, project(): pl.pallas_call(body, in_specs=specs, out_specs=out_specs, out_shape=shape...  45.4 us
    ppermute x30, waiting for transfers between devices, swap(): return lax.ppermute(x, axis, [(i, i ^ mask) for i in range(size)])  43.4 us
    ppermute x30, starting transfers between devices, swap(): return lax.ppermute(x, axis, [(i, i ^ mask) for i in range(size)])  24.1 us
    pallas_call x1, Pallas kernels, step_project(): pl.pallas_call(step_kernel, grid_spec=pltpu.PrefetchScalarGridSpec(num_sc...  14.3 us
    all_to_all x1, starting transfers between devices, per_device(): lax.all_to_all(held, 'tp', split_axis=0, concat_axis=0, tiled=True)  9.86 us
    pallas_call x1, Pallas kernels, prefill_attention(): pl.pallas_call(prefill_kernel, in_specs=[vmem()] * 4, out_specs=vmem(), o...  9.5 us
    ppermute x5, starting transfers between devices, ring_y(): lax.ppermute(x, 'tp', [(i, (i + 4) % TP if i % 2 == 0 else (i - 4) % TP)...  8.7 us
  transfers between devices with their start and end apart: 38, of which 13 were waited for; matrix products, arithmetic and copies ran while one was open for 16% of the time, Pallas kernels for 45%

profile of v1, /device:TPU:10, one launch (start us, length us, event | category | flops | bytes accessed | tf_op | source)
XLA Modules:
  0.0 291.2 jit_solution(13668918120500574257)
XLA Ops:
  2.7 0.8 fusion.26
  3.5 0.7 multiply_add_fusion
  4.9 0.9 pad_maximum_fusion.5
  5.8 8.3 %all-to-all-start = ((bf16[8,80,512]{2,1,0:T(8,128)(2,1)}), bf16[8,80,512]{2,1,0:T(8,128)(2,1)S(1)}, u32[]{:S(2)}, u32[]{:S(2)}) async-start(bf16[8,80,512]{2,1,0:T(8,128)(2,1)} %pad_maximum_fusion.5), calls=%async_computation | async-start | bytes 1310720 | tf_op jit(solution)/shard_map/all_to_all | solution.py:613
  14.2 3.0 %collective-permute-start.29 = (s32[1,33,128]{2,1,0:T(8,128)S(1)}, s32[1,33,128]{2,1,0:T(8,128)S(1)}, u32[]{:S(2)}, u32[]{:S(2)}) collective-permute-start(s32[1,33,128]{2,1,0:T(8,128)S(1)} %bitcast.113), channel_id=1, source_target_pairs={{0,64},{16,80},{32,96},{48,112},{64,0},{80,16},{96,32},{112,48},{1... | collective-permute-start | bytes 50696 | tf_op jit(solution)/shard_map/ppermute | solution.py:45
  19.9 2.6 select_reduce_fusion.1
  26.3 0.9 collective-permute-done.30
  27.2 3.4 %collective-permute-start.31 = (s32[4,33,128]{2,1,0:T(8,128)S(1)}, s32[4,33,128]{2,1,0:T(8,128)S(1)}, u32[]{:S(2)}, u32[]{:S(2)}) collective-permute-start(s32[4,33,128]{2,1,0:T(8,128)S(1)} %pad_add_fusion.1), channel_id=1, source_target_pairs={{0,48},{16,32},{32,16},{48,0},{64,112},{80,96},{96,80},{112,64},{1... | collective-permute-start | bytes 202760 | tf_op jit(solution)/shard_map/ppermute | solution.py:45
  31.3 1.0 collective-permute-start.13
  33.3 1.7 select_reduce_fusion
  36.5 0.7 pad_maximum_fusion.10
  38.4 2.5 multiply_reduce_fusion
  40.9 1.3 multiply_reduce_fusion.1
  42.2 1.0 collective-permute-start
  43.8 0.9 pad_maximum_fusion.7
  44.7 1.9 collective-permute-start.15
  47.4 0.7 select_reduce_fusion.3
  48.1 1.0 collective-permute-start.26
  49.1 8.1 %collective-permute-done = bf16[512,512]{1,0:T(8,128)(2,1)} collective-permute-done((bf16[512,512]{1,0:T(8,128)(2,1)}, bf16[512,512]{1,0:T(8,128)(2,1)}, u32[]{:S(2)}, u32[]{:S(2)}) %collective-permute-start) | collective-permute-done | bytes 524320 | tf_op jit(solution)/shard_map/ppermute | solution.py:45
  57.9 1.3 pad_maximum_fusion.1.refs_6_
  59.2 2.7 collective-permute-start.6
  61.9 2.3 pad_maximum_fusion.2.refs_2_
  64.2 0.7 collective-permute-start.8
  65.0 1.1 constant_dynamic-update-slice_fusion.xs
  66.1 2.0 collective-permute-done.26
  68.1 2.1 pad_maximum_fusion.refs_3_
  70.2 2.4 collective-permute-start.2
  72.6 1.3 copy-done.2
  73.9 14.3 %step_project.1 = (bf16[64,512]{1,0:T(8,128)(2,1)}, bf16[64,128]{1,0:T(8,128)(2,1)}, bf16[64,128]{1,0:T(8,128)(2,1)}) custom-call(s32[16]{0:T(128)} %broadcast_xor_fusion.1.order, bf16[16,64,512]{2,1,0:T(8,128)(2,1)} %copy-done.8, bf16[16,1,512]{2,1,0:T(2,128)(2,1)} %reshape.430.gain.refs_11_.refs_7_, bf16[8192,512]{1,0:T(8,128)(2,1)} %refs_8_.1, ...), custom_call_target="tpu_custom_call" | custom-call | flops 805306368 | bytes 14680064 | tf_op jit(solution)/shard_map/step_project/pallas_call | solution.py:157
  88.2 0.9 reshape.421
  89.3 2.3 pad_maximum_fusion.4.refs_7_
  91.9 1.1 slice.99
  93.0 1.1 slice.100
  94.1 1.1 collective-permute-start.18
  95.3 0.8 collective-permute-start.9
  96.1 1.5 collective-permute-done.32
  97.6 1.9 collective-permute-start.33
  99.5 0.7 collective-permute-done.18
  100.2 1.2 collective-permute-start.19
  101.4 1.0 collective-permute-start.23
  102.9 2.2 collective-permute-start.34
  105.1 11.4 %collective-permute-done.19 = bf16[4,288,128]{2,1,0:T(8,128)(2,1)S(1)} collective-permute-done((bf16[4,288,128]{2,1,0:T(8,128)(2,1)S(1)}, bf16[4,288,128]{2,1,0:T(8,128)(2,1)S(1)}, u32[]{:S(2)}, u32[]{:S(2)}) %collective-permute-start.19) | collective-permute-done | bytes 294944 | tf_op jit(solution)/shard_map/ppermute | solution.py:45
  117.3 1.1 slice_bitcast_fusion
  118.4 2.1 collective-permute-start.3
  120.4 0.8 pad_maximum_fusion.8.q
  121.3 11.6 %collective-permute-done.20 = bf16[8,288,128]{2,1,0:T(8,128)(2,1)S(1)} collective-permute-done((bf16[8,288,128]{2,1,0:T(8,128)(2,1)S(1)}, bf16[8,288,128]{2,1,0:T(8,128)(2,1)S(1)}, u32[]{:S(2)}, u32[]{:S(2)}) %collective-permute-start.20) | collective-permute-done | bytes 589856 | tf_op jit(solution)/shard_map/ppermute | solution.py:45
  132.9 2.4 fusion.44
  136.1 1.1 slice.106.q
  138.5 52.9 %paged_attention.1 = bf16[16,272,128]{2,1,0:T(8,128)(2,1)} custom-call(s32[17]{0:T(128)} %copy-done.25, s32[256]{0:T(256)} %get-tuple-element.17.slot_page, s32[256]{0:T(256)} %get-tuple-element.16.slot_live, s32[16]{0:T(128)} %fusion.34.where, bf16[16,256,128]{2,1,0:T(8,128)(2,1)} %slice.106.q, bf16[128,16,2048]{2,1,0:T(8,128)(2,1)} %cache.1), custom_call_target="tpu_custom_call" | custom-call | flops 2000000000 | bytes 12582912 | tf_op jit(solution)/shard_map/paged_attention/pallas_call | solution.py:383
  191.4 9.9 %all-to-all-start.1 = ((bf16[16,272,128]{2,1,0:T(8,128)(2,1)}), bf16[16,272,128]{2,1,0:T(8,128)(2,1)S(1)}, u32[]{:S(2)}, u32[]{:S(2)}) async-start(bf16[16,272,128]{2,1,0:T(8,128)(2,1)} %paged_attention.1), calls=%async_computation.1 | async-start | bytes 2228224 | tf_op jit(solution)/shard_map/all_to_all | solution.py:740
  201.5 1.5 collective-permute-start.10
  203.0 18.4 %prefill_project.3.refs_15_ = f32[1024,768]{1,0:T(8,128)} custom-call(s32[8]{0:T(128)} %stack.131.refs_0_, s32[1]{0:T(128)} %bitcast.2.refs_1_, bf16[2,512,512]{2,1,0:T(8,128)(2,1)} %pad_maximum_fusion.2.refs_2_, bf16[2,512,512]{2,1,0:T(8,128)(2,1)} %pad_maximum_fusion.refs_3_, bf16[2,512,512]{2,1,0:T(8,128)(2,1)} %collective-permute-done.8.refs_4_, ...), custom_call_target="tpu_custom_call" | custom-call | flops 6442450944 | bytes 16777216 | tf_op jit(solution)/shard_map/prefill_project/pallas_call | solution.py:302
  221.4 5.7 %collective-permute-done.10 = bf16[512,512]{1,0:T(8,128)(2,1)S(1)} collective-permute-done((bf16[512,512]{1,0:T(8,128)(2,1)}, bf16[512,512]{1,0:T(8,128)(2,1)S(1)}, u32[]{:S(2)}, u32[]{:S(2)}) %collective-permute-start.10) | collective-permute-done | bytes 524320 | tf_op jit(solution)/shard_map/ppermute | solution.py:45
  227.1 2.4 fusion.43
  229.5 18.2 %prefill_project.4.refs_11_ = f32[1024,768]{1,0:T(8,128)} custom-call(s32[6]{0:T(128)} %stack.122.refs_0_, s32[1]{0:T(128)} %bitcast.2.refs_1_, bf16[2,512,512]{2,1,0:T(8,128)(2,1)} %collective-permute-done.2.refs_2_, bf16[2,512,512]{2,1,0:T(8,128)(2,1)} %collective-permute-done.21.refs_3_, bf16[1,512,512]{2,1,0:T(8,128)(2,1)} %get-tuple-element.26.refs_4_, ...), custom_call_target="tpu_custom_call" | custom-call | flops 4831838208 | bytes 12582912 | tf_op jit(solution)/shard_map/prefill_project/pallas_call | solution.py:302
  247.8 0.8 copy-done.15
  248.8 8.7 %prefill_project.5 = (bf16[1024,512]{1,0:T(8,128)(2,1)}, bf16[1024,128]{1,0:T(8,128)(2,1)}, bf16[1024,128]{1,0:T(8,128)(2,1)}) custom-call(s32[2]{0:T(128)} %pad_add_fusion.5.refs_0_, s32[1]{0:T(128)} %bitcast.2.refs_1_, bf16[1,512,512]{2,1,0:T(8,128)(2,1)} %bitcast.105, bf16[1,512,512]{2,1,0:T(8,128)(2,1)} %bitcast.106, bf16[1,512,512]{2,1,0:T(8,128)(2,1)} %bitcast.107, ...), custom_call_target="tpu_custom_call" | custom-call | flops 1610612736 | bytes 4194304 | tf_op jit(solution)/shard_map/prefill_project/pallas_call | solution.py:302
  257.5 8.2 %fresh_attention.1 = bf16[8,272,128]{2,1,0:T(8,128)(2,1)} custom-call(s32[8]{0:T(128)} %broadcast_xor_fusion.group, bf16[8,256,128]{2,1,0:T(8,128)(2,1)} %pad_maximum_fusion.8.q, bf16[1024,128]{1,0:T(8,128)(2,1)} %get-tuple-element.10.keys, bf16[1024,128]{1,0:T(8,128)(2,1)} %get-tuple-element.11.values, s32[1,1024]{1,0:T(1,128)} %select_n.295.token_row), custom_call_target="tpu_custom_call" | custom-call | flops 1000000000 | bytes 2097152 | tf_op jit(solution)/shard_map/fresh_attention/pallas_call | solution.py:424
  265.7 7.5 %all-to-all-start.2 = ((bf16[8,272,128]{2,1,0:T(8,128)(2,1)}), bf16[8,272,128]{2,1,0:T(8,128)(2,1)S(1)}, u32[]{:S(2)}, u32[]{:S(2)}) async-start(bf16[8,272,128]{2,1,0:T(8,128)(2,1)} %fresh_attention.1), calls=%async_computation.2 | async-start | bytes 1114112 | tf_op jit(solution)/shard_map/all_to_all | solution.py:745
  273.8 9.5 %prefill_attention.1 = bf16[1024,512]{1,0:T(8,128)(2,1)} custom-call(bf16[1024,512]{1,0:T(8,128)(2,1)} %get-tuple-element.9.q, bf16[1024,128]{1,0:T(8,128)(2,1)} %get-tuple-element.10.keys, bf16[1024,128]{1,0:T(8,128)(2,1)} %get-tuple-element.11.values, f32[1,1024]{1,0:T(1,128)} %bitcast.133), custom_call_target="tpu_custom_call" | custom-call | flops 3000000000 | bytes 3145728 | tf_op jit(solution)/shard_map/prefill_attention/pallas_call | solution.py:460
  283.3 1.1 all-to-all-done.2.fresh
  284.5 0.8 copy-done.6
  285.3 4.4 %decode_merge.1 = bf16[256,128]{1,0:T(8,128)(2,1)} custom-call(bf16[16,272,128]{2,1,0:T(8,128)(2,1)} %copy-done.3, bf16[8,272,128]{2,1,0:T(8,128)(2,1)} %copy-done.6, bf16[256,128]{1,0:T(8,128)(2,1)} %bitcast.88, bf16[64,128]{1,0:T(8,128)(2,1)} %get-tuple-element.28.new_keys, bf16[64,128]{1,0:T(8,128)(2,1)} %get-tuple-element.27.new_values), custom_call_target="tpu_custom_call" | custom-call | flops 10000000 | bytes 2097152 | tf_op jit(solution)/shard_map/decode_merge/pallas_call | solution.py:500
  289.7 0.9 reshape.429
  (195 shorter events, 21.2 us)
Async XLA Ops:
  0.6 3.8 %copy-start = (bf16[256,512]{1,0:T(8,128)(2,1)S(1)}, bf16[256,512]{1,0:T(8,128)(2,1)}, u32[]{:S(2)}) copy-start(bf16[256,512]{1,0:T(8,128)(2,1)} %param.16) | copy-start | bytes 786436
  0.6 30.0 %collective-permute-start.12 = (bf16[1,64,512]{2,1,0:T(8,128)(2,1)}, bf16[1,64,512]{2,1,0:T(8,128)(2,1)S(1)}, u32[]{:S(2)}, u32[]{:S(2)}) collective-permute-start(bf16[1,64,512]{2,1,0:T(8,128)(2,1)} %bitcast.97), channel_id=1, source_target_pairs={{0,1},{1,0},{2,3},{3,2},{4,5},{5,4},{6,7},{7,6},{8,9},{9,8},{10,11... | collective-permute-start | bytes 196616 | tf_op jit(solution)/shard_map/ppermute | solution.py:45
  0.7 71.9 %collective-permute-start.16 = (bf16[8192,128]{1,0:T(8,128)(2,1)}, bf16[8192,128]{1,0:T(8,128)(2,1)S(1)}, u32[]{:S(2)}, u32[]{:S(2)}) collective-permute-start(bf16[8192,128]{1,0:T(8,128)(2,1)} %refs_9_.1), channel_id=1, source_target_pairs={{0,1},{1,0},{2,3},{3,2},{4,5},{5,4},{6,7},{7,6},{8,9},{9,8},{10,11... | collective-permute-start | bytes 6291464 | tf_op jit(solution)/shard_map/ppermute | solution.py:45
  4.8 9.3 %copy-start.19 = (s32[16,256]{1,0:T(8,128)S(1)}, s32[16,256]{1,0:T(8,128)}, u32[]{:S(2)}) copy-start(s32[16,256]{1,0:T(8,128)} %param.22) | copy-start | bytes 49156
  4.8 9.3 %copy-start.23 = (s32[64]{0:T(128)S(1)}, s32[64]{0:T(128)}, u32[]{:S(2)}) copy-start(s32[64]{0:T(128)} %param.20) | copy-start | bytes 772
  4.8 9.3 %copy-start.24 = (s32[16]{0:T(128)S(1)}, s32[16]{0:T(128)}, u32[]{:S(2)}) copy-start(s32[16]{0:T(128)} %param.23) | copy-start | bytes 196
  4.8 12.3 %copy-start.13 = (bf16[4,16,512]{2,1,0:T(8,128)(2,1)S(1)}, bf16[4,16,512]{2,1,0:T(8,128)(2,1)}, u32[]{:S(2)}) copy-start(bf16[4,16,512]{2,1,0:T(8,128)(2,1)} %param.24) | copy-start | bytes 196612
  4.8 13.1 %copy-start.29 = (s32[8]{0:T(128)S(1)}, s32[8]{0:T(128)}, u32[]{:S(2)}) copy-start(s32[8]{0:T(128)} %constant.241.clone) | copy-start | bytes 100
  4.8 13.6 %copy-start.28 = (s32[16]{0:T(128)S(1)}, s32[16]{0:T(128)}, u32[]{:S(2)}) copy-start(s32[16]{0:T(128)} %constant.240.clone) | copy-start | bytes 196
  4.9 14.2 %copy-start.27 = (s32[1,8]{1,0:T(1,128)S(1)}, s32[1,8]{1,0:T(1,128)}, u32[]{:S(2)}) copy-start(s32[1,8]{1,0:T(1,128)} %param.19) | copy-start | bytes 100
  5.8 18.7 %copy-start.20 = (bf16[8192]{0:T(1024)(128)(2,1)S(1)}, bf16[8192]{0:T(1024)(128)(2,1)}, u32[]{:S(2)}) copy-start(bf16[8192]{0:T(1024)(128)(2,1)} %param.25) | copy-start | bytes 49156
  5.8 31.9 %all-to-all-start = ((bf16[8,80,512]{2,1,0:T(8,128)(2,1)}), bf16[8,80,512]{2,1,0:T(8,128)(2,1)S(1)}, u32[]{:S(2)}, u32[]{:S(2)}) async-start(bf16[8,80,512]{2,1,0:T(8,128)(2,1)} %pad_maximum_fusion.5), calls=%async_computation | async-start | bytes 1310720 | tf_op jit(solution)/shard_map/all_to_all | solution.py:613
  14.2 8.9 %collective-permute-start.29 = (s32[1,33,128]{2,1,0:T(8,128)S(1)}, s32[1,33,128]{2,1,0:T(8,128)S(1)}, u32[]{:S(2)}, u32[]{:S(2)}) collective-permute-start(s32[1,33,128]{2,1,0:T(8,128)S(1)} %bitcast.113), channel_id=1, source_target_pairs={{0,64},{16,80},{32,96},{48,112},{64,0},{80,16},{96,32},{112,48},{1... | collective-permute-start | bytes 50696 | tf_op jit(solution)/shard_map/ppermute | solution.py:45
  23.1 4.1 %collective-permute-start.30 = (s32[2,33,128]{2,1,0:T(8,128)S(1)}, s32[2,33,128]{2,1,0:T(8,128)S(1)}, u32[]{:S(2)}, u32[]{:S(2)}) collective-permute-start(s32[2,33,128]{2,1,0:T(8,128)S(1)} %pad_add_fusion.2), channel_id=1, source_target_pairs={{0,16},{16,0},{32,48},{48,32},{64,80},{80,64},{96,112},{112,96},{1... | collective-permute-start | bytes 101384 | tf_op jit(solution)/shard_map/ppermute | solution.py:45
  27.2 5.8 %collective-permute-start.31 = (s32[4,33,128]{2,1,0:T(8,128)S(1)}, s32[4,33,128]{2,1,0:T(8,128)S(1)}, u32[]{:S(2)}, u32[]{:S(2)}) collective-permute-start(s32[4,33,128]{2,1,0:T(8,128)S(1)} %pad_add_fusion.1), channel_id=1, source_target_pairs={{0,48},{16,32},{32,16},{48,0},{64,112},{80,96},{96,80},{112,64},{1... | collective-permute-start | bytes 202760 | tf_op jit(solution)/shard_map/ppermute | solution.py:45
  31.3 5.2 %collective-permute-start.13 = (bf16[2,64,512]{2,1,0:T(8,128)(2,1)}, bf16[2,64,512]{2,1,0:T(8,128)(2,1)S(1)}, u32[]{:S(2)}, u32[]{:S(2)}) collective-permute-start(bf16[2,64,512]{2,1,0:T(8,128)(2,1)} %pad_maximum_fusion.13), channel_id=1, source_target_pairs={{0,2},{1,3},{2,0},{3,1},{4,6},{5,7},{6,4},{7,5},{8,10},{9,11},{10,... | collective-permute-start | bytes 393224 | tf_op jit(solution)/shard_map/ppermute | solution.py:45
  35.9 5.0 %copy-start.25 = (s32[17]{0:T(128)}, s32[17]{0:T(128)S(1)}, u32[]{:S(2)}) copy-start(s32[17]{0:T(128)S(1)} %select_reduce_fusion.8.first_chunk) | copy-start | bytes 208
  37.3 6.6 %collective-permute-start.14 = (bf16[4,64,512]{2,1,0:T(8,128)(2,1)}, bf16[4,64,512]{2,1,0:T(8,128)(2,1)S(1)}, u32[]{:S(2)}, u32[]{:S(2)}) collective-permute-start(bf16[4,64,512]{2,1,0:T(8,128)(2,1)} %pad_maximum_fusion.10), channel_id=1, source_target_pairs={{0,4},{1,5},{2,6},{3,7},{4,0},{5,1},{6,2},{7,3},{8,12},{9,13},{10,... | collective-permute-start | bytes 786440 | tf_op jit(solution)/shard_map/ppermute | solution.py:45
  38.4 2.5 copy-start.26
  40.9 7.3 %collective-permute-start.5 = (bf16[512,512]{1,0:T(8,128)(2,1)}, bf16[512,512]{1,0:T(8,128)(2,1)S(1)}, u32[]{:S(2)}, u32[]{:S(2)}) collective-permute-start(bf16[512,512]{1,0:T(8,128)(2,1)} %get-tuple-element.30), channel_id=1, source_target_pairs={{0,1},{1,0},{2,3},{3,2},{4,5},{5,4},{6,7},{7,6},{8,9},{9,8},{10,11... | collective-permute-start | bytes 1572872 | tf_op jit(solution)/shard_map/ppermute | solution.py:45
  42.2 15.0 %collective-permute-start = (bf16[512,512]{1,0:T(8,128)(2,1)}, bf16[512,512]{1,0:T(8,128)(2,1)}, u32[]{:S(2)}, u32[]{:S(2)}) collective-permute-start(bf16[512,512]{1,0:T(8,128)(2,1)} %get-tuple-element.32), channel_id=1, source_target_pairs={{0,2},{1,3},{2,0},{3,1},{4,6},{5,7},{6,4},{7,5},{8,10},{9,11},{10,... | collective-permute-start | bytes 1572872 | tf_op jit(solution)/shard_map/ppermute | solution.py:45
  43.8 14.0 %copy-start.11 = (bf16[4,64,512]{2,1,0:T(8,128)(2,1)}, bf16[4,64,512]{2,1,0:T(8,128)(2,1)S(1)}, u32[]{:S(2)}) copy-start(bf16[4,64,512]{2,1,0:T(8,128)(2,1)S(1)} %collective-permute-done.14) | copy-start | bytes 786436
  44.7 19.5 %collective-permute-start.15 = (bf16[8,64,512]{2,1,0:T(8,128)(2,1)}, bf16[8,64,512]{2,1,0:T(8,128)(2,1)}, u32[]{:S(2)}, u32[]{:S(2)}) collective-permute-start(bf16[8,64,512]{2,1,0:T(8,128)(2,1)} %pad_maximum_fusion.7), channel_id=1, source_target_pairs={{0,12},{1,13},{2,14},{3,15},{4,8},{5,9},{6,10},{7,11},{8,4},{9,5},... | collective-permute-start | bytes 1572872 | tf_op jit(solution)/shard_map/ppermute | solution.py:45
  46.7 12.5 %collective-permute-start.7 = (bf16[512,512]{1,0:T(8,128)(2,1)}, bf16[512,512]{1,0:T(8,128)(2,1)}, u32[]{:S(2)}, u32[]{:S(2)}) collective-permute-start(bf16[512,512]{1,0:T(8,128)(2,1)} %get-tuple-element.32), channel_id=1, source_target_pairs={{0,1},{1,0},{2,3},{3,2},{4,5},{5,4},{6,7},{7,6},{8,9},{9,8},{10,11... | collective-permute-start | bytes 1572872 | tf_op jit(solution)/shard_map/ppermute | solution.py:45
  48.1 9.8 %copy-start.18 = (bf16[512,512]{1,0:T(8,128)(2,1)}, bf16[512,512]{1,0:T(8,128)(2,1)S(1)}, u32[]{:S(2)}) copy-start(bf16[512,512]{1,0:T(8,128)(2,1)S(1)} %collective-permute-done.5) | copy-start | bytes 1572868
  48.1 19.9 %collective-permute-start.26 = (bf16[512,512]{1,0:T(8,128)(2,1)}, bf16[512,512]{1,0:T(8,128)(2,1)}, u32[]{:S(2)}, u32[]{:S(2)}) collective-permute-start(bf16[512,512]{1,0:T(8,128)(2,1)} %get-tuple-element.30), channel_id=1, source_target_pairs={{0,2},{1,3},{2,0},{3,1},{4,6},{5,7},{6,4},{7,5},{8,10},{9,11},{10,... | collective-permute-start | bytes 1572872 | tf_op jit(solution)/shard_map/ppermute | solution.py:45
  57.2 10.9 %collective-permute-start.1 = (bf16[512,512]{1,0:T(8,128)(2,1)}, bf16[512,512]{1,0:T(8,128)(2,1)S(1)}, u32[]{:S(2)}, u32[]{:S(2)}) collective-permute-start(bf16[512,512]{1,0:T(8,128)(2,1)} %collective-permute-done), channel_id=1, source_target_pairs={{0,1},{1,0},{2,3},{3,2},{4,5},{5,4},{6,7},{7,6},{8,9},{9,8},{10,11... | collective-permute-start | bytes 1572872 | tf_op jit(solution)/shard_map/ppermute | solution.py:45
  59.2 5.8 %copy-start.4 = (bf16[2,512,512]{2,1,0:T(8,128)(2,1)}, bf16[2,512,512]{2,1,0:T(8,128)(2,1)S(1)}, u32[]{:S(2)}) copy-start(bf16[2,512,512]{2,1,0:T(8,128)(2,1)S(1)} %pad_maximum_fusion.1.refs_6_) | copy-start | bytes 3145732
  59.2 5.7 %copy-start.7 = (bf16[16,64,512]{2,1,0:T(8,128)(2,1)S(1)}, bf16[16,64,512]{2,1,0:T(8,128)(2,1)}, u32[]{:S(2)}) copy-start(bf16[16,64,512]{2,1,0:T(8,128)(2,1)} %constant_dynamic-update-slice_fusion.2) | copy-start | bytes 3145732
  59.2 5.7 %copy-start.12 = (bf16[4,64,512]{2,1,0:T(8,128)(2,1)S(1)}, bf16[4,64,512]{2,1,0:T(8,128)(2,1)}, u32[]{:S(2)}) copy-start(bf16[4,64,512]{2,1,0:T(8,128)(2,1)} %copy-done.11) | copy-start | bytes 786436
  59.2 32.7 %collective-permute-start.6 = (bf16[2,512,512]{2,1,0:T(8,128)(2,1)S(1)}, bf16[2,512,512]{2,1,0:T(8,128)(2,1)}, u32[]{:S(2)}, u32[]{:S(2)}) collective-permute-start(bf16[2,512,512]{2,1,0:T(8,128)(2,1)S(1)} %pad_maximum_fusion.1.refs_6_), channel_id=1, source_target_pairs={{0,4},{1,13},{2,6},{3,15},{4,8},{5,1},{6,10},{7,3},{8,12},{9,5},{1... | collective-permute-start | bytes 3145736 | tf_op jit(solution)/shard_map/ppermute | solution.py:49
  64.2 28.8 %collective-permute-start.8 = (bf16[2,512,512]{2,1,0:T(8,128)(2,1)}, bf16[2,512,512]{2,1,0:T(8,128)(2,1)}, u32[]{:S(2)}, u32[]{:S(2)}) collective-permute-start(bf16[2,512,512]{2,1,0:T(8,128)(2,1)} %pad_maximum_fusion.2.refs_2_), channel_id=1, source_target_pairs={{0,4},{1,13},{2,6},{3,15},{4,8},{5,1},{6,10},{7,3},{8,12},{9,5},{1... | collective-permute-start | bytes 3145736 | tf_op jit(solution)/shard_map/ppermute | solution.py:49
  66.1 6.5 %copy-start.8 = (bf16[16,64,512]{2,1,0:T(8,128)(2,1)}, bf16[16,64,512]{2,1,0:T(8,128)(2,1)S(1)}, u32[]{:S(2)}) copy-start(bf16[16,64,512]{2,1,0:T(8,128)(2,1)S(1)} %constant_dynamic-update-slice_fusion.xs) | copy-start | bytes 3145732
  68.1 21.2 %collective-permute-start.27 = (bf16[512,512]{1,0:T(8,128)(2,1)}, bf16[512,512]{1,0:T(8,128)(2,1)}, u32[]{:S(2)}, u32[]{:S(2)}) collective-permute-start(bf16[512,512]{1,0:T(8,128)(2,1)} %collective-permute-done.26), channel_id=1, source_target_pairs={{0,1},{1,0},{2,3},{3,2},{4,5},{5,4},{6,7},{7,6},{8,9},{9,8},{10,11... | collective-permute-start | bytes 1572872 | tf_op jit(solution)/shard_map/ppermute | solution.py:45
  70.2 46.6 %collective-permute-start.2 = (bf16[2,512,512]{2,1,0:T(8,128)(2,1)}, bf16[2,512,512]{2,1,0:T(8,128)(2,1)}, u32[]{:S(2)}, u32[]{:S(2)}) collective-permute-start(bf16[2,512,512]{2,1,0:T(8,128)(2,1)} %pad_maximum_fusion.refs_3_), channel_id=1, source_target_pairs={{0,4},{1,13},{2,6},{3,15},{4,8},{5,1},{6,10},{7,3},{8,12},{9,5},{1... | collective-permute-start | bytes 3145736 | tf_op jit(solution)/shard_map/ppermute | solution.py:49
  72.6 1.3 copy-start.2
  89.1 31.3 %copy-start.5 = (bf16[4,16,4,128]{3,2,0,1:T(4,128)(2,1)}, bf16[4,16,4,128]{3,2,0,1:T(4,128)(2,1)S(1)}, u32[]{:S(2)}) copy-start(bf16[4,16,4,128]{3,2,0,1:T(4,128)(2,1)S(1)} %copy.32) | copy-start | bytes 196612
  89.2 4.9 %collective-permute-start.17 = (bf16[1,288,128]{2,1,0:T(8,128)(2,1)S(1)}, bf16[1,288,128]{2,1,0:T(8,128)(2,1)S(1)}, u32[]{:S(2)}, u32[]{:S(2)}) collective-permute-start(bf16[1,288,128]{2,1,0:T(8,128)(2,1)S(1)} %bitcast.90), channel_id=1, source_target_pairs={{0,1},{1,0},{2,3},{3,2},{4,5},{5,4},{6,7},{7,6},{8,9},{9,8},{10,11... | collective-permute-start | bytes 221192 | tf_op jit(solution)/shard_map/ppermute | solution.py:45
  91.6 6.0 %collective-permute-start.32 = (bf16[1,256,128]{2,1,0:T(8,128)(2,1)S(1)}, bf16[1,256,128]{2,1,0:T(8,128)(2,1)S(1)}, u32[]{:S(2)}, u32[]{:S(2)}) collective-permute-start(bf16[1,256,128]{2,1,0:T(8,128)(2,1)S(1)} %bitcast.84), channel_id=1, source_target_pairs={{0,64},{16,80},{32,96},{48,112},{64,0},{80,16},{96,32},{112,48},{1... | collective-permute-start | bytes 196616 | tf_op jit(solution)/shard_map/ppermute | solution.py:45
  94.1 6.0 %collective-permute-start.18 = (bf16[2,288,128]{2,1,0:T(8,128)(2,1)S(1)}, bf16[2,288,128]{2,1,0:T(8,128)(2,1)S(1)}, u32[]{:S(2)}, u32[]{:S(2)}) collective-permute-start(bf16[2,288,128]{2,1,0:T(8,128)(2,1)S(1)} %pad_maximum_fusion.12), channel_id=1, source_target_pairs={{0,2},{1,3},{2,0},{3,1},{4,6},{5,7},{6,4},{7,5},{8,10},{9,11},{10,... | collective-permute-start | bytes 442376 | tf_op jit(solution)/shard_map/ppermute | solution.py:45
  95.3 23.1 %collective-permute-start.9 = (bf16[2,512,512]{2,1,0:T(8,128)(2,1)S(1)}, bf16[2,512,512]{2,1,0:T(8,128)(2,1)}, u32[]{:S(2)}, u32[]{:S(2)}) collective-permute-start(bf16[2,512,512]{2,1,0:T(8,128)(2,1)S(1)} %pad_maximum_fusion.3), channel_id=1, source_target_pairs={{0,4},{1,13},{2,6},{3,15},{4,8},{5,1},{6,10},{7,3},{8,12},{9,5},{1... | collective-permute-start | bytes 3145736 | tf_op jit(solution)/shard_map/ppermute | solution.py:49
  97.6 5.2 %collective-permute-start.33 = (bf16[2,256,128]{2,1,0:T(8,128)(2,1)S(1)}, bf16[2,256,128]{2,1,0:T(8,128)(2,1)S(1)}, u32[]{:S(2)}, u32[]{:S(2)}) collective-permute-start(bf16[2,256,128]{2,1,0:T(8,128)(2,1)S(1)} %pad_maximum_fusion.14), channel_id=1, source_target_pairs={{0,16},{16,0},{32,48},{48,32},{64,80},{80,64},{96,112},{112,96},{1... | collective-permute-start | bytes 393224 | tf_op jit(solution)/shard_map/ppermute | solution.py:45
  100.2 16.3 %collective-permute-start.19 = (bf16[4,288,128]{2,1,0:T(8,128)(2,1)S(1)}, bf16[4,288,128]{2,1,0:T(8,128)(2,1)S(1)}, u32[]{:S(2)}, u32[]{:S(2)}) collective-permute-start(bf16[4,288,128]{2,1,0:T(8,128)(2,1)S(1)} %pad_maximum_fusion.9), channel_id=1, source_target_pairs={{0,4},{1,5},{2,6},{3,7},{4,0},{5,1},{6,2},{7,3},{8,12},{9,13},{10,... | collective-permute-start | bytes 884744 | tf_op jit(solution)/shard_map/ppermute | solution.py:45
  101.4 36.3 %collective-permute-start.23 = (bf16[2,512,512]{2,1,0:T(8,128)(2,1)}, bf16[2,512,512]{2,1,0:T(8,128)(2,1)S(1)}, u32[]{:S(2)}, u32[]{:S(2)}) collective-permute-start(bf16[2,512,512]{2,1,0:T(8,128)(2,1)} %collective-permute-done.6.refs_8_), channel_id=1, source_target_pairs={{0,2},{1,3},{2,0},{3,1},{4,6},{5,7},{6,4},{7,5},{8,10},{9,11},{10,... | collective-permute-start | bytes 3145736 | tf_op jit(solution)/shard_map/ppermute | solution.py:45
  102.9 13.8 %collective-permute-start.34 = (bf16[4,256,128]{2,1,0:T(8,128)(2,1)S(1)}, bf16[4,256,128]{2,1,0:T(8,128)(2,1)S(1)}, u32[]{:S(2)}, u32[]{:S(2)}) collective-permute-start(bf16[4,256,128]{2,1,0:T(8,128)(2,1)S(1)} %pad_maximum_fusion.11), channel_id=1, source_target_pairs={{0,48},{16,32},{32,16},{48,0},{64,112},{80,96},{96,80},{112,64},{1... | collective-permute-start | bytes 786440 | tf_op jit(solution)/shard_map/ppermute | solution.py:45
  116.5 16.3 %collective-permute-start.20 = (bf16[8,288,128]{2,1,0:T(8,128)(2,1)S(1)}, bf16[8,288,128]{2,1,0:T(8,128)(2,1)S(1)}, u32[]{:S(2)}, u32[]{:S(2)}) collective-permute-start(bf16[8,288,128]{2,1,0:T(8,128)(2,1)S(1)} %pad_maximum_fusion.6), channel_id=1, source_target_pairs={{0,12},{1,13},{2,14},{3,15},{4,8},{5,9},{6,10},{7,11},{8,4},{9,5},... | collective-permute-start | bytes 1769480 | tf_op jit(solution)/shard_map/ppermute | solution.py:45
  116.7 84.6 %collective-permute-start.28 = (bf16[2,512,512]{2,1,0:T(8,128)(2,1)}, bf16[2,512,512]{2,1,0:T(8,128)(2,1)S(1)}, u32[]{:S(2)}, u32[]{:S(2)}) collective-permute-start(bf16[2,512,512]{2,1,0:T(8,128)(2,1)} %collective-permute-done.6.refs_8_), channel_id=1, source_target_pairs={{0,1},{1,0},{2,3},{3,2},{4,5},{5,4},{6,7},{7,6},{8,9},{9,8},{10,11... | collective-permute-start | bytes 3145736 | tf_op jit(solution)/shard_map/ppermute | solution.py:45
  116.8 84.7 %collective-permute-start.25 = (bf16[2,512,512]{2,1,0:T(8,128)(2,1)}, bf16[2,512,512]{2,1,0:T(8,128)(2,1)}, u32[]{:S(2)}, u32[]{:S(2)}) collective-permute-start(bf16[2,512,512]{2,1,0:T(8,128)(2,1)} %collective-permute-done.8.refs_4_), channel_id=1, source_target_pairs={{0,1},{1,0},{2,3},{3,2},{4,5},{5,4},{6,7},{7,6},{8,9},{9,8},{10,11... | collective-permute-start | bytes 3145736 | tf_op jit(solution)/shard_map/ppermute | solution.py:45
  118.4 18.8 %collective-permute-start.3 = (bf16[512,512]{1,0:T(8,128)(2,1)S(1)}, bf16[512,512]{1,0:T(8,128)(2,1)S(1)}, u32[]{:S(2)}, u32[]{:S(2)}) collective-permute-start(bf16[512,512]{1,0:T(8,128)(2,1)S(1)} %slice_bitcast_fusion), channel_id=1, source_target_pairs={{0,4},{1,13},{2,6},{3,15},{4,8},{5,1},{6,10},{7,3},{8,12},{9,5},{1... | collective-permute-start | bytes 1572872 | tf_op jit(solution)/shard_map/ppermute | solution.py:49
  132.9 94.2 %collective-permute-start.22 = (bf16[2,512,512]{2,1,0:T(8,128)(2,1)}, bf16[2,512,512]{2,1,0:T(8,128)(2,1)}, u32[]{:S(2)}, u32[]{:S(2)}) collective-permute-start(bf16[2,512,512]{2,1,0:T(8,128)(2,1)} %collective-permute-done.9), channel_id=1, source_target_pairs={{0,1},{1,0},{2,3},{3,2},{4,5},{5,4},{6,7},{7,6},{8,9},{9,8},{10,11... | collective-permute-start | bytes 3145736 | tf_op jit(solution)/shard_map/ppermute | solution.py:45
  137.2 92.4 %collective-permute-start.21 = (bf16[2,512,512]{2,1,0:T(8,128)(2,1)}, bf16[2,512,512]{2,1,0:T(8,128)(2,1)}, u32[]{:S(2)}, u32[]{:S(2)}) collective-permute-start(bf16[2,512,512]{2,1,0:T(8,128)(2,1)} %collective-permute-done.2.refs_2_), channel_id=1, source_target_pairs={{0,1},{1,0},{2,3},{3,2},{4,5},{5,4},{6,7},{7,6},{8,9},{9,8},{10,11... | collective-permute-start | bytes 3145736 | tf_op jit(solution)/shard_map/ppermute | solution.py:45
  138.0 53.4 %copy-start.9 = (bf16[2,512,512]{2,1,0:T(8,128)(2,1)}, bf16[2,512,512]{2,1,0:T(8,128)(2,1)S(1)}, u32[]{:S(2)}) copy-start(bf16[2,512,512]{2,1,0:T(8,128)(2,1)S(1)} %collective-permute-done.23.refs_6_) | copy-start | bytes 3145732
  138.0 91.6 %collective-permute-start.24 = (bf16[2,512,512]{2,1,0:T(8,128)(2,1)S(1)}, bf16[2,512,512]{2,1,0:T(8,128)(2,1)}, u32[]{:S(2)}, u32[]{:S(2)}) collective-permute-start(bf16[2,512,512]{2,1,0:T(8,128)(2,1)S(1)} %collective-permute-done.23.refs_6_), channel_id=1, source_target_pairs={{0,1},{1,0},{2,3},{3,2},{4,5},{5,4},{6,7},{7,6},{8,9},{9,8},{10,11... | collective-permute-start | bytes 3145736 | tf_op jit(solution)/shard_map/ppermute | solution.py:45
  191.4 74.3 %all-to-all-start.1 = ((bf16[16,272,128]{2,1,0:T(8,128)(2,1)}), bf16[16,272,128]{2,1,0:T(8,128)(2,1)S(1)}, u32[]{:S(2)}, u32[]{:S(2)}) async-start(bf16[16,272,128]{2,1,0:T(8,128)(2,1)} %paged_attention.1), calls=%async_computation.1 | async-start | bytes 2228224 | tf_op jit(solution)/shard_map/all_to_all | solution.py:740
  201.3 1.7 copy-start.10
  201.3 46.5 %collective-permute-start.4 = (bf16[512,512]{1,0:T(8,128)(2,1)}, bf16[512,512]{1,0:T(8,128)(2,1)S(1)}, u32[]{:S(2)}, u32[]{:S(2)}) collective-permute-start(bf16[512,512]{1,0:T(8,128)(2,1)} %copy-done.14), channel_id=1, source_target_pairs={{0,1},{1,0},{2,3},{3,2},{4,5},{5,4},{6,7},{7,6},{8,9},{9,8},{10,11... | collective-permute-start | bytes 1572872 | tf_op jit(solution)/shard_map/ppermute | solution.py:45
  201.5 25.6 %collective-permute-start.10 = (bf16[512,512]{1,0:T(8,128)(2,1)}, bf16[512,512]{1,0:T(8,128)(2,1)S(1)}, u32[]{:S(2)}, u32[]{:S(2)}) collective-permute-start(bf16[512,512]{1,0:T(8,128)(2,1)} %get-tuple-element.25), channel_id=1, source_target_pairs={{0,2},{1,3},{2,0},{3,1},{4,6},{5,7},{6,4},{7,5},{8,10},{9,11},{10,... | collective-permute-start | bytes 1572872 | tf_op jit(solution)/shard_map/ppermute | solution.py:45
  227.1 20.7 %copy-start.16 = (bf16[512,512]{1,0:T(8,128)(2,1)}, bf16[512,512]{1,0:T(8,128)(2,1)S(1)}, u32[]{:S(2)}) copy-start(bf16[512,512]{1,0:T(8,128)(2,1)S(1)} %collective-permute-done.10) | copy-start | bytes 1572868
  227.1 20.7 %collective-permute-start.11 = (bf16[512,512]{1,0:T(8,128)(2,1)S(1)}, bf16[512,512]{1,0:T(8,128)(2,1)S(1)}, u32[]{:S(2)}, u32[]{:S(2)}) collective-permute-start(bf16[512,512]{1,0:T(8,128)(2,1)S(1)} %collective-permute-done.10), channel_id=1, source_target_pairs={{0,1},{1,0},{2,3},{3,2},{4,5},{5,4},{6,7},{7,6},{8,9},{9,8},{10,11... | collective-permute-start | bytes 1572872 | tf_op jit(solution)/shard_map/ppermute | solution.py:45
  257.4 15.8 %copy-start.21 = (bf16[64,128]{1,0:T(8,128)(2,1)S(1)}, bf16[64,128]{1,0:T(8,128)(2,1)}, u32[]{:S(2)}) copy-start(bf16[64,128]{1,0:T(8,128)(2,1)} %get-tuple-element.12) | copy-start | bytes 49156
  257.5 15.8 %copy-start.22 = (bf16[64,128]{1,0:T(8,128)(2,1)S(1)}, bf16[64,128]{1,0:T(8,128)(2,1)}, u32[]{:S(2)}) copy-start(bf16[64,128]{1,0:T(8,128)(2,1)} %get-tuple-element.13) | copy-start | bytes 49156
  265.7 17.7 %copy-start.3 = (bf16[16,272,128]{2,1,0:T(8,128)(2,1)}, bf16[16,272,128]{2,1,0:T(8,128)(2,1)S(1)}, u32[]{:S(2)}) copy-start(bf16[16,272,128]{2,1,0:T(8,128)(2,1)S(1)} %all-to-all-done.1.held) | copy-start | bytes 3342340
  265.7 18.8 %all-to-all-start.2 = ((bf16[8,272,128]{2,1,0:T(8,128)(2,1)}), bf16[8,272,128]{2,1,0:T(8,128)(2,1)S(1)}, u32[]{:S(2)}, u32[]{:S(2)}) async-start(bf16[8,272,128]{2,1,0:T(8,128)(2,1)} %fresh_attention.1), calls=%async_computation.2 | async-start | bytes 1114112 | tf_op jit(solution)/shard_map/all_to_all | solution.py:745
  273.8 17.3 %copy-start.1 = (bf16[256,512]{1,0:T(8,128)(2,1)S(1)}, bf16[256,512]{1,0:T(8,128)(2,1)}, u32[]{:S(2)}) copy-start(bf16[256,512]{1,0:T(8,128)(2,1)} %param.16) | copy-start | bytes 786436
  (4 other events, 3.4 us)
